TPU v7x, 256 devices: a whole 4x4x8 slice. The times are simulated.
256 devices in a mesh: key: 128 (over y, z, x), feat: 2 (over core).
Axes of the slice: x: 4, y: 4, z: 8, core: 2. Of those that a mesh axis runs over, the one named last changes fastest.
Arguments:
- partials: bfloat16 [8192, 64, 384], P('key', 'feat'), may hold values from -6 to 6
- dest_key: int32 [8192], P('key'), may hold values from 0 to 16383, as said below
- active_from: int32 [16384], P('key'), may hold values from 0 to 383
- cohort: int32 [16384], P('key'), may hold values from 0 to 15, as said below
- decay_rate: float32 [3, 64], P(None, 'feat'), may hold values from 0.01 to 0.7
Outputs:
- windowed: bfloat16 [16384, 3, 64, 384], P('key', None, 'feat')
- cohort_mean: float32 [16, 3, 64, 384], P(None, None, 'feat', 'key')
Inputs may be any that keep to these rules, and one draw needn't show every extreme that they name: `dest_key`: owner of key k is k // 128. The 64 rows of one device name at most one key of any one owner; in every draw some owner gets exactly 1 row from every device. Cohort sizes are uneven, and a cohort may have no keys.
All inputs are finite; a program needn't handle non-finite values.
Results may differ from a plain program's by a relative error of at most 0.012.
Values may be sent and summed in bfloat16 or wider, within the bound.
A program may use at most 192 MiB of HBM per device.

v0:
```python
import jax
import jax.numpy as jnp
from jax import lax
from jax.sharding import PartitionSpec as P

CAP = 1
FEAT = 64
BLOCK = 128
WIN_A = 7
WIN_B = 28
WIN_C = 91
COHORTS = 16


def band_table(decay_rates):
    source_day = jnp.arange(2 * BLOCK)[:, None]
    target_day = jnp.arange(BLOCK)[None, :]
    lag_days = (BLOCK + target_day - source_day).astype(jnp.float32)
    columns = []
    for window_idx, window_len in enumerate((WIN_A, WIN_B, WIN_C)):
        in_band = (lag_days >= 0) & (lag_days < window_len)
        weights = jnp.exp(-decay_rates[window_idx][:, None, None] * lag_days[None])
        columns.append(jnp.where(in_band[None], weights, 0.0))
    return jnp.concatenate(columns, axis=2).astype(jnp.bfloat16)


def on_device(partials, dest_key, active_from, cohort, decay_rate):
    key_devs = lax.axis_size("key")
    row_count, feat_count, day_count = partials.shape
    key_count = active_from.shape[0]
    slot_count = key_devs * CAP
    owner_dev = dest_key // key_count
    local_key = dest_key % key_count
    owner_hot = (owner_dev[:, None] == jnp.arange(key_devs)[None, :]).astype(jnp.int32)
    slot_rank = jnp.sum(jnp.cumsum(owner_hot, axis=0) * owner_hot, axis=1) - 1
    slot_index = owner_dev * CAP + slot_rank
    select = slot_index[None, :] == jnp.arange(slot_count)[:, None]
    packed = jnp.dot(
        select.astype(jnp.bfloat16),
        partials.reshape(row_count, -1),
        preferred_element_type=jnp.float32,
    )
    packed = packed.astype(jnp.bfloat16).reshape(slot_count, feat_count, day_count)
    slot_local = jnp.sum(jnp.where(select, local_key[None, :] + 1, 0), axis=1) - 1
    arrived = lax.all_to_all(slot_local, "key", split_axis=0, concat_axis=0, tiled=True)
    receive = (arrived[None, :] == jnp.arange(key_count)[:, None]).astype(jnp.bfloat16)
    live_mask = (jnp.arange(day_count)[None, :] >= active_from[:, None]).astype(jnp.float32)
    rows = lax.all_to_all(packed, "key", split_axis=0, concat_axis=0, tiled=True)
    items = rows.shape[1]
    summed = jnp.dot(receive, rows.reshape(rows.shape[0], -1), preferred_element_type=jnp.float32)
    summed = summed.reshape(key_count, items, day_count)
    daily = (summed * live_mask[:, None, :]).astype(jnp.bfloat16)
    band_weights = band_table(decay_rate)
    blocks = day_count // BLOCK
    padded = jnp.concatenate(
        [jnp.zeros((key_count, feat_count, BLOCK), jnp.bfloat16), daily], axis=2
    )
    pieces = jnp.stack(
        [
            padded[:, :, block_idx * BLOCK : block_idx * BLOCK + 2 * BLOCK]
            for block_idx in range(blocks)
        ],
        axis=2,
    )
    raw_window = jnp.einsum(
        "kfji,fio->kfjo", pieces, band_weights, preferred_element_type=jnp.float32
    )
    raw_window = raw_window.reshape(key_count, feat_count, blocks, 3, BLOCK).transpose(
        0, 3, 1, 2, 4
    )
    raw_window = raw_window.reshape(key_count, 3, feat_count, day_count).astype(jnp.bfloat16)
    raw_float = raw_window.astype(jnp.float32)
    squares = jnp.sum(jnp.square(raw_float), axis=(2, 3))
    key_total = lax.psum(squares, "feat")
    norm_scale = lax.rsqrt(key_total / (FEAT * day_count) + 1e-05)
    windowed = (raw_float * norm_scale[:, :, None, None]).astype(jnp.bfloat16)
    member = cohort[None, :] == jnp.arange(COHORTS)[:, None]
    part_table = jnp.dot(
        member.astype(jnp.bfloat16),
        windowed.reshape(key_count, -1),
        preferred_element_type=jnp.float32,
    )
    part_table = part_table.reshape(COHORTS, 3, feat_count, day_count)
    part_count = jnp.sum(member.astype(jnp.float32), axis=1)
    day_share = day_count // key_devs
    whole_table, whole_count = lax.psum((part_table, part_count), "key")
    own_days = lax.dynamic_slice_in_dim(
        whole_table, lax.axis_index("key") * day_share, day_share, 3
    )
    cohort_count = whole_count[:, None, None, None]
    cohort_mean = own_days / jnp.maximum(cohort_count, 1.0)
    return (windowed, cohort_mean)


def solution(mesh):
    placed = (P("key", "feat", None), P("key"), P("key"), P("key"), P(None, "feat"))
    return jax.shard_map(
        on_device,
        mesh=mesh,
        in_specs=placed,
        out_specs=(P("key", None, "feat", None), P(None, None, "feat", "key")),
        check_vma=False,
    )
```

profile of v0, /device:TPU:2, one launch (start us, length us, event | category | flops | bytes accessed | tf_op | source)
XLA Modules:
  0.0 585.9 jit_solution(1641966483915755649)
XLA Ops:
  7.2 0.7 fusion.29
  7.8 0.1 fusion.23
  7.9 0.1 reduce_window_sum.11
  8.0 0.2 select_reduce_fusion.1
  8.2 0.1 select_reduce_fusion
  8.3 0.7 copy.29
  9.1 15.4 %all-to-all-start = ((s32[128,1,1]{2,1,0:T(1,128)}), s32[128,1,1]{2,1,0:T(1,128)S(1)}, u32[]{:S(2)}, u32[]{:S(2)}) async-start(s32[128,1,1]{2,1,0:T(1,128)} %copy.29), calls=%async_computation | async-start | bytes 131072 | tf_op jit(solution)/shard_map/all_to_all | solution.py:45
  24.5 2.0 copy.38
  26.5 1.1 convolution_convert_fusion
  27.6 2.3 copy.39
  29.9 0.0 copy-start.3
  29.9 0.0 copy-start.4
  29.9 5.7 all-to-all-done
  35.6 8.3 %all-to-all-start.1 = ((bf16[128,32,384]{2,1,0:T(8,128)(2,1)}), bf16[128,32,384]{2,1,0:T(8,128)(2,1)S(1)}, u32[]{:S(2)}, u32[]{:S(2)}) async-start(bf16[128,32,384]{2,1,0:T(8,128)(2,1)} %bitcast.37), calls=%async_computation.1 | async-start | bytes 6291456 | tf_op jit(solution)/shard_map/all_to_all | solution.py:48
  43.8 0.2 all-reduce.3.cloned.1.call-start
  44.1 0.0 copy-done.3
  44.1 0.2 fusion.19
  44.2 0.1 subtract_convert_fusion
  44.3 0.0 copy-done.4
  44.3 0.1 fusion.12
  44.4 3.7 select_convert_fusion.2
  48.1 2.3 reduce.5
  50.5 67.2 %all-to-all-done.1 = bf16[128,32,384]{2,1,0:T(8,128)(2,1)S(1)} async-done(((bf16[128,32,384]{2,1,0:T(8,128)(2,1)}), bf16[128,32,384]{2,1,0:T(8,128)(2,1)S(1)}, u32[]{:S(2)}, u32[]{:S(2)}) %all-to-all-start.1) | async-done | bytes 3145760 | tf_op jit(solution)/shard_map/all_to_all | solution.py:48
  117.6 3.2 copy.37
  120.9 2.9 multiply_convert_fusion
  123.8 0.0 copy-start
  123.8 0.0 copy-start.1
  123.8 0.0 copy-start.2
  123.8 2.9 fusion.11
  126.7 0.0 copy-done
  126.7 0.4 copy-done.1
  127.1 1.0 copy-done.2
  128.1 9.8 %multiply_reduce_fusion = (f32[384,128]{1,0:T(8,128)S(1)}, f32[32,384,128,3]{2,1,3,0:T(8,128)}) fusion(bf16[32,256,128]{1,2,0:T(8,128)(2,1)S(1)} %copy-done.2, bf16[32,256,128]{1,2,0:T(8,128)(2,1)S(1)} %copy-done.1, bf16[32,256,128]{1,2,0:T(8,128)(2,1)S(1)} %copy-done, bf16[128,32,1,256]{3,0,1,2:T(8,128)(2,1)} %get-tuple-element.13, ...), kind=kOutput, calls=%fused_computation.4 | convolution fusion | flops 2459910144 | bytes 31653888 | tf_op jit(solution)/shard_map/kfji,fio->kfjo/dot_general | solution.py:65
  138.0 12.8 %copy.32 = f32[128,32,3,3,128]{0,4,2,1,3:T(8,128)} copy(f32[128,32,3,3,128]{0,4,3,2,1:T(8,128)} %bitcast.67) | data formatting | bytes 37748736 | tf_op jit(solution)/shard_map/convert_element_type | solution.py:72
  150.8 2.5 psum.21
  153.3 0.0 copy-start.5
  153.3 42.8 %fusion = bf16[128,36864]{0,1:T(8,128)(2,1)S(1)} fusion(f32[128,32,3,3,128]{0,4,2,1,3:T(8,128)} %copy.32, f32[128,3]{0,1:T(4,128)S(1)} %add_rsqrt_fusion), kind=kLoop, calls=%fused_computation.1 | loop fusion | flops 9437184 | bytes 28313088 | tf_op jit(solution)/shard_map/convert_element_type | solution.py:76
  196.1 0.0 copy-done.5
  196.1 7.8 %fusion.26 = f32[16,3,32,384]{0,3,2,1:T(8,128)} fusion(bf16[3,32,384,128]{3,2,1,0:T(8,128)(2,1)S(1)} %bitcast.66, s32[128]{0:T(128)S(1)} %copy-done.5), kind=kOutput, calls=%fused_computation.47 | convolution fusion | flops 150996992 | bytes 11796992 | tf_op jit(solution)/shard_map/dot_general | solution.py:78
  204.0 0.0 all-reduce.3.cloned.1.call-update
  204.0 0.1 convert_reduce_fusion
  204.1 348.7 %psum.23 = f32[16]{0:T(128)S(1)} all-reduce(f32[16]{0:T(128)S(1)} %convert_reduce_fusion), channel_id=1, replica_groups=mesh['key'=128,'feat'=2] {'key'}, use_global_device_ids=true, to_apply=%region_7.8 | all-reduce | flops 16 | bytes 128 | tf_op jit(solution)/shard_map/psum | solution.py:86
  552.9 11.6 %fusion.1 = bf16[128,3,32,384]{0,3,2,1:T(8,128)(2,1)} fusion(f32[128,32,3,3,128]{0,4,2,1,3:T(8,128)} %copy.32, f32[128,3]{0,1:T(4,128)S(1)} %add_rsqrt_fusion), kind=kLoop, calls=%fused_computation.3 | loop fusion | flops 9437184 | bytes 28313088 | tf_op jit(solution)/shard_map/convert_element_type | solution.py:76
  564.5 12.7 %copy.33 = bf16[128,3,32,384]{3,2,1,0:T(8,128)(2,1)} copy(bf16[128,3,32,384]{0,3,2,1:T(8,128)(2,1)} %fusion.1) | data formatting | bytes 18874368
  577.2 0.0 all-reduce.3.cloned.1.call-done
  577.2 1.2 dynamic-slice_divide_fusion
  578.4 0.7 copy.34
  (7 shorter events, 0.1 us)
Async XLA Ops:
  9.1 26.5 %all-to-all-start = ((s32[128,1,1]{2,1,0:T(1,128)}), s32[128,1,1]{2,1,0:T(1,128)S(1)}, u32[]{:S(2)}, u32[]{:S(2)}) async-start(s32[128,1,1]{2,1,0:T(1,128)} %copy.29), calls=%async_computation | async-start | bytes 131072 | tf_op jit(solution)/shard_map/all_to_all | solution.py:45
  29.9 14.2 %copy-start.3 = (f32[3,32]{1,0:T(4,128)S(1)}, f32[3,32]{1,0:T(4,128)}, u32[]{:S(2)}) copy-start(f32[3,32]{1,0:T(4,128)} %param.9) | copy-start | bytes 1156
  29.9 14.5 %copy-start.4 = (s32[128]{0:T(128)S(1)}, s32[128]{0:T(128)}, u32[]{:S(2)}) copy-start(s32[128]{0:T(128)} %param.7) | copy-start | bytes 1540
  35.6 82.1 %all-to-all-start.1 = ((bf16[128,32,384]{2,1,0:T(8,128)(2,1)}), bf16[128,32,384]{2,1,0:T(8,128)(2,1)S(1)}, u32[]{:S(2)}, u32[]{:S(2)}) async-start(bf16[128,32,384]{2,1,0:T(8,128)(2,1)} %bitcast.37), calls=%async_computation.1 | async-start | bytes 6291456 | tf_op jit(solution)/shard_map/all_to_all | solution.py:48
  43.8 533.3 %all-reduce.3.cloned.1.call-start = ((), (), s32[]{:S(2)}) async-start(), calls=%async_computation.2 | async-start | bytes 37748736 | tf_op jit(solution)/shard_map/psum | solution.py:86
  123.8 2.9 copy-start
  123.8 3.3 copy-start.1
  123.8 4.4 copy-start.2
  153.3 42.8 %copy-start.5 = (s32[128]{0:T(128)S(1)}, s32[128]{0:T(128)}, u32[]{:S(2)}) copy-start(s32[128]{0:T(128)} %param.8) | copy-start | bytes 1540
Sparse Core Ops, SparseCore 0:
  204.1 360.4 all-reduce.2
where the time goes:
time: 589 us; the launch traced here: 586 us
  blocking collectives  351 us (60%)
  waiting for transfers between devices  72.9 us (12%)
  other arithmetic  63.2 us (11%)
  local copies, waits for them, and re-layouts  38.9 us (7%)
  starting transfers between devices  23.9 us (4%)
  matrix products  21.7 us (4%)
  between operations  14.2 us (2%)
    psum x1, blocking collectives, on_device(): whole_table, whole_count = lax.psum((part_table, part_count), 'key')  349 us
    all_to_all x1, waiting for transfers between devices, on_device(): lax.all_to_all(packed, 'key', split_axis=0, concat_axis=0, tiled=True)  67.2 us
    convert_element_type x2, other arithmetic, on_device(): windowed = (raw_float * norm_scale[:, :, None, None]).astype(jnp.bfloat16)  54.4 us
    unnamed x16, local copies, waits for them, and re-layouts  19.2 us
    all_to_all x1, starting transfers between devices, on_device(): lax.all_to_all(slot_local, 'key', split_axis=0, concat_axis=0, tiled=True)  15.4 us
    convert_element_type x1, local copies, waits for them, and re-layouts, on_device(): raw_float = raw_window.astype(jnp.float32)  12.8 us
  transfers between devices with their start and end apart: 3, of which 2 were waited for; matrix products, arithmetic and copies ran while one was open for 6% of the time, Pallas kernels for 0%

commit v1 on v0

--- a/solution.py
+++ b/solution.py
@@ -1,6 +1,10 @@
+import functools
+
 import jax
 import jax.numpy as jnp
 from jax import lax
+from jax.experimental import pallas as pl
+from jax.experimental.pallas import tpu as pltpu
 from jax.sharding import PartitionSpec as P
 
 CAP = 1
@@ -10,6 +14,8 @@
 WIN_B = 28
 WIN_C = 91
 COHORTS = 16
+NY, NZ, NX = 4, 8, 4
+MESH = pl.DeviceIdType.MESH
 
 
 def band_table(decay_rates):
@@ -24,28 +30,94 @@
     return jnp.concatenate(columns, axis=2).astype(jnp.bfloat16)
 
 
+def peer_at(me, step):
+    y, z, x = me // (NZ * NX), (me // NX) % NZ, me % NX
+    dy, dz, dx = step // (NZ * NX), (step // NX) % NZ, step % NX
+    return ((y + dy) % NY) * (NZ * NX) + ((z + dz) % NZ) * NX + (x + dx) % NX
+
+
+def exchange_kernel(peers, rows_ref, slot_ref, out_ref, held, packed, send_sem, recv_sem, own_sem):
+    me = lax.axis_index("key")
+    load = pltpu.make_async_copy(rows_ref, held, own_sem)
+    load.start()
+    barrier = pltpu.get_barrier_semaphore()
+
+    def greet(step, carry):
+        pl.semaphore_signal(barrier, 1, device_id={"key": peer_at(me, step)}, device_id_type=MESH)
+        return carry
+
+    lax.fori_loop(1, peers, greet, 0)
+    load.wait()
+    packed[0] = held[slot_ref[me]]
+    own = pltpu.make_async_copy(packed.at[0], out_ref.at[me], own_sem)
+    own.start()
+    pl.semaphore_wait(barrier, peers - 1)
+
+    def send(step, carry):
+        peer = peer_at(me, step)
+        packed[step] = held[slot_ref[peer]]
+        pltpu.make_async_remote_copy(
+            src_ref=packed.at[step],
+            dst_ref=out_ref.at[me],
+            send_sem=send_sem,
+            recv_sem=recv_sem,
+            device_id={"key": peer},
+            device_id_type=MESH,
+        ).start()
+        return carry
+
+    lax.fori_loop(1, peers, send, 0)
+    own.wait()
+    whole = pltpu.make_async_remote_copy(
+        src_ref=packed.at[pl.ds(1, peers - 1)],
+        dst_ref=out_ref.at[pl.ds(0, peers - 1)],
+        send_sem=send_sem,
+        recv_sem=recv_sem,
+        device_id={"key": peer_at(me, 1)},
+        device_id_type=MESH,
+    )
+    whole.wait_send()
+    whole.wait_recv()
+
+
+def exchange(partials, slot_row, peers):
+    rows, feats, days = partials.shape
+    return pl.pallas_call(
+        functools.partial(exchange_kernel, peers),
+        out_shape=jax.ShapeDtypeStruct((peers, feats, days), partials.dtype),
+        in_specs=[
+            pl.BlockSpec(memory_space=pl.ANY),
+            pl.BlockSpec(memory_space=pltpu.SMEM),
+        ],
+        out_specs=pl.BlockSpec(memory_space=pl.ANY),
+        scratch_shapes=[
+            pltpu.VMEM((rows, feats, days), partials.dtype),
+            pltpu.VMEM((peers, feats, days), partials.dtype),
+            pltpu.SemaphoreType.DMA,
+            pltpu.SemaphoreType.DMA,
+            pltpu.SemaphoreType.DMA,
+        ],
+        compiler_params=pltpu.CompilerParams(
+            collective_id=0, has_side_effects=True, vmem_limit_bytes=32 << 20
+        ),
+        cost_estimate=pl.CostEstimate(flops=0, bytes_accessed=200_000_000, transcendentals=0),
+    )(partials, slot_row)
+
+
 def on_device(partials, dest_key, active_from, cohort, decay_rate):
     key_devs = lax.axis_size("key")
     row_count, feat_count, day_count = partials.shape
     key_count = active_from.shape[0]
-    slot_count = key_devs * CAP
+    me = lax.axis_index("key")
     owner_dev = dest_key // key_count
-    local_key = dest_key % key_count
-    owner_hot = (owner_dev[:, None] == jnp.arange(key_devs)[None, :]).astype(jnp.int32)
-    slot_rank = jnp.sum(jnp.cumsum(owner_hot, axis=0) * owner_hot, axis=1) - 1
-    slot_index = owner_dev * CAP + slot_rank
-    select = slot_index[None, :] == jnp.arange(slot_count)[:, None]
-    packed = jnp.dot(
-        select.astype(jnp.bfloat16),
-        partials.reshape(row_count, -1),
-        preferred_element_type=jnp.float32,
-    )
-    packed = packed.astype(jnp.bfloat16).reshape(slot_count, feat_count, day_count)
-    slot_local = jnp.sum(jnp.where(select, local_key[None, :] + 1, 0), axis=1) - 1
-    arrived = lax.all_to_all(slot_local, "key", split_axis=0, concat_axis=0, tiled=True)
+    match = owner_dev[None, :] == jnp.arange(key_devs)[:, None]
+    slot_row = jnp.sum(jnp.where(match, jnp.arange(row_count)[None, :], 0), axis=1).astype(jnp.int32)
+    all_dest = lax.all_gather(dest_key, "key")
+    rows = exchange(partials, slot_row, key_devs)
+    mine = (all_dest // key_count) == me
+    arrived = jnp.sum(jnp.where(mine, all_dest % key_count + 1, 0), axis=1) - 1
     receive = (arrived[None, :] == jnp.arange(key_count)[:, None]).astype(jnp.bfloat16)
     live_mask = (jnp.arange(day_count)[None, :] >= active_from[:, None]).astype(jnp.float32)
-    rows = lax.all_to_all(packed, "key", split_axis=0, concat_axis=0, tiled=True)
     items = rows.shape[1]
     summed = jnp.dot(receive, rows.reshape(rows.shape[0], -1), preferred_element_type=jnp.float32)
     summed = summed.reshape(key_count, items, day_count)
@@ -80,15 +152,13 @@
         windowed.reshape(key_count, -1),
         preferred_element_type=jnp.float32,
     )
-    part_table = part_table.reshape(COHORTS, 3, feat_count, day_count)
+    part_table = part_table.reshape(COHORTS * 3 * feat_count, day_count)
     part_count = jnp.sum(member.astype(jnp.float32), axis=1)
+    whole_count = lax.psum(part_count, "key")
+    own_days = lax.psum_scatter(part_table.T, "key", scatter_dimension=0, tiled=True)
     day_share = day_count // key_devs
-    whole_table, whole_count = lax.psum((part_table, part_count), "key")
-    own_days = lax.dynamic_slice_in_dim(
-        whole_table, lax.axis_index("key") * day_share, day_share, 3
-    )
-    cohort_count = whole_count[:, None, None, None]
-    cohort_mean = own_days / jnp.maximum(cohort_count, 1.0)
+    own_days = own_days.T.reshape(COHORTS, 3, feat_count, day_share)
+    cohort_mean = own_days / jnp.maximum(whole_count, 1.0)[:, None, None, None]
     return (windowed, cohort_mean)
 
 

time: 589 us -> 1200 us (2.04)
  blocking collectives: 351 us -> 1040 us
  waiting for transfers between devices: 72.9 us -> 0.02 us
  Pallas kernels: 0 us -> 47.9 us
  other arithmetic: 63.2 us -> 32.4 us
  starting transfers between devices: 23.9 us -> 0.04 us
    unnamed x0 -> x1, blocking collectives: none -> 696 us
    all_to_all x2 -> x0, waiting for transfers between devices: 72.9 us -> none  [the longest x1 67.2 us: on_device(): lax.all_to_all(packed, 'key', split_axis=0, concat_axis=0, tiled=True)]
    pallas_call x0 -> x1, Pallas kernels: none -> 47.9 us  [exchange(): pl.pallas_call(functools.partial(exchange_kernel, peers), out_shape=jax.S...]
    convert_element_type x2, other arithmetic: 54.4 us -> 26.4 us  [on_device(): windowed = (raw_float * norm_scale[:, :, None, None]).astype(jnp.bfloat16)]
    all_to_all x2 -> x0, starting transfers between devices: 23.7 us -> none  [the longest x1 15.4 us: on_device(): lax.all_to_all(slot_local, 'key', split_axis=0, concat_axis=0, tiled=True)]
    unnamed x16 -> x14, local copies, waits for them, and re-layouts: 19.2 us -> 26.4 us
  transfers between devices with their start and end apart: 3 -> 1, of which waited for: 2 -> 0; matrix products, arithmetic and copies ran while one was open for 6% -> 2% of each run, Pallas kernels for 0% -> 0%
where the time goes in v1:
time: 1200 us
  blocking collectives  1040 us (87%)
  Pallas kernels  47.9 us (4%)
  local copies, waits for them, and re-layouts  46 us (4%)
  other arithmetic  32.4 us (3%)
  between operations  15.4 us (1%)
  matrix products  13.4 us (1%)
    unnamed x1, blocking collectives  696 us
    psum x1, blocking collectives, on_device(): whole_count = lax.psum(part_count, 'key')  344 us
    pallas_call x1, Pallas kernels, exchange(): pl.pallas_call(functools.partial(exchange_kernel, peers), out_shape=jax.S...  47.9 us
    unnamed x14, local copies, waits for them, and re-layouts  26.4 us
    convert_element_type x2, other arithmetic, on_device(): windowed = (raw_float * norm_scale[:, :, None, None]).astype(jnp.bfloat16)  26.4 us
  transfers between devices with their start and end apart: 1, of which 0 were waited for; matrix products, arithmetic and copies ran while one was open for 2% of the time, Pallas kernels for 0%

profile of v1, /device:TPU:2, one launch (start us, length us, event | category | flops | bytes accessed | tf_op | source)
XLA Modules:
  0.0 1197.0 jit_solution(11760201182289192431)
XLA Ops:
  7.2 0.0 all-reduce.5.cloned.1.call-start
  7.2 0.8 fusion.15
  8.0 0.1 subtract_convert_fusion
  8.1 0.7 and_select_fusion
  8.8 0.1 select_reduce_fusion.slot_ref
  8.9 0.8 negate_bitcast_fusion.2
  9.7 1.3 fusion.28
  11.7 0.9 dynamic-update-slice
  12.6 695.8 %all-reduce.1 = s32[8192]{0:T(1024)S(1)} all-reduce(s32[8192]{0:T(1024)S(1)} %dynamic-update-slice), channel_id=2, replica_groups=mesh['key'=128,'feat'=2] {'key'}, use_global_device_ids=true, to_apply=%add.1 | all-reduce | flops 8192 | bytes 65536
  708.4 0.1 reshape.180
  708.4 0.1 fusion.19
  708.6 0.7 fusion.8
  709.3 0.0 copy-start
  709.3 1.4 copy-done
  710.7 47.9 %shard_map.68 = bf16[128,32,384]{2,1,0:T(8,128)(2,1)S(1)} custom-call(bf16[64,32,384]{2,1,0:T(8,128)(2,1)S(1)} %copy-done, s32[128]{0:T(128)S(1)} %select_reduce_fusion.slot_ref), custom_call_target="tpu_custom_call" | custom-call | bytes 200000000 | tf_op jit(solution)/shard_map/pallas_call | solution.py:85
  758.7 3.0 copy.29
  761.7 3.5 copy.22
  765.2 1.0 multiply_convert_fusion
  766.1 0.0 copy-start.2
  766.2 2.8 fusion.7
  768.9 0.0 copy-done.2
  768.9 2.5 select_convert_fusion.2
  771.4 9.9 multiply_reduce_fusion
  781.3 2.5 psum.14
  783.8 7.5 copy.24
  791.3 0.0 copy-start.1
  791.3 6.5 copy-done.1
  797.8 0.0 copy-start.3
  797.8 14.5 %fusion = bf16[128,36864]{0,1:T(8,128)(2,1)S(1)} fusion(f32[128,32,3,3,128]{0,4,2,1,3:T(8,128)S(1)} %copy.24, f32[128,3]{0,1:T(4,128)S(1)} %add_rsqrt_fusion), kind=kLoop, calls=%fused_computation.1 | loop fusion | flops 9437184 | bytes 28313088 | tf_op jit(solution)/shard_map/convert_element_type | solution.py:148
  812.3 0.0 copy-done.3
  812.3 2.5 fusion.25
  814.8 1.6 reshape.172
  816.4 3.1 copy.25
  819.5 0.0 all-reduce.5.cloned.1.call-update
  819.5 11.8 fusion.1
  831.4 12.7 %copy.26 = bf16[128,3,32,384]{3,2,1,0:T(8,128)(2,1)} copy(bf16[128,3,32,384]{0,3,2,1:T(8,128)(2,1)} %fusion.1) | data formatting | bytes 18874368
  844.7 0.1 convert_reduce_fusion
  844.8 343.6 %psum.15 = f32[16]{0:T(128)S(1)} all-reduce(f32[16]{0:T(128)S(1)} %convert_reduce_fusion), channel_id=1, replica_groups=mesh['key'=128,'feat'=2] {'key'}, use_global_device_ids=true, to_apply=%region_6.7 | all-reduce | flops 16 | bytes 128 | tf_op jit(solution)/shard_map/psum | solution.py:157
  1188.4 0.0 all-reduce.5.cloned.1.call-done
  1188.4 0.9 dynamic-slice_bitcast_fusion
  1189.3 0.1 reshape.173
  1189.5 0.1 broadcast_divide_fusion
  1189.6 0.6 copy.27
  (6 shorter events, 0.1 us)
Async XLA Ops:
  7.2 1181.3 %all-reduce.5.cloned.1.call-start = ((), (), s32[]{:S(2)}) async-start(), calls=%async_computation | async-start | bytes 4718592
  709.3 1.4 copy-start
  766.1 2.8 copy-start.2
  791.3 6.5 copy-start.1
  797.8 14.5 %copy-start.3 = (s32[128]{0:T(128)S(1)}, s32[128]{0:T(128)}, u32[]{:S(2)}) copy-start(s32[128]{0:T(128)} %param.8) | copy-start | bytes 1540
Sparse Core Ops, SparseCore 0:
  819.6 226.8 all-reduce.4

commit v2 on v1

v2 whole, which is shorter than its diff:
```python
import functools

import jax
import jax.numpy as jnp
from jax import lax
from jax.experimental import pallas as pl
from jax.experimental.pallas import tpu as pltpu
from jax.sharding import PartitionSpec as P

FEAT = 64
BLOCK = 128
WINDOWS = (7, 28, 91)
COHORTS = 16
NY, NZ, NX = 4, 8, 4
PLANE = NY * NX
MESH = pl.DeviceIdType.MESH


def peer_at(me, step):
    y, z, x = me // (NZ * NX), (me // NX) % NZ, me % NX
    dy, dz, dx = step // (NZ * NX), (step // NX) % NZ, step % NX
    return ((y + dy) % NY) * (NZ * NX) + ((z + dz) % NZ) * NX + (x + dx) % NX


def exchange_kernel(
    peers, rows_ref, slot_ref, note_ref, out_ref, got_ref, held, packed, sems
):
    me = lax.axis_index("key")
    load = pltpu.make_async_copy(rows_ref, held, sems.at[0])
    load.start()
    barrier = pltpu.get_barrier_semaphore()

    def greet(step, carry):
        pl.semaphore_signal(barrier, 1, device_id={"key": peer_at(me, step)}, device_id_type=MESH)
        return carry

    lax.fori_loop(1, peers, greet, 0)
    load.wait()
    packed[0] = held[slot_ref[me]]
    own = pltpu.make_async_copy(packed.at[0], out_ref.at[me], sems.at[0])
    own.start()
    own_note = pltpu.make_async_copy(note_ref.at[me], got_ref.at[me], sems.at[5])
    own_note.start()
    pl.semaphore_wait(barrier, peers - 1)

    def send(step, carry):
        peer = peer_at(me, step)
        packed[step] = held[slot_ref[peer]]
        pltpu.make_async_remote_copy(
            src_ref=packed.at[step],
            dst_ref=out_ref.at[me],
            send_sem=sems.at[1],
            recv_sem=sems.at[2],
            device_id={"key": peer},
            device_id_type=MESH,
        ).start()
        pltpu.make_async_remote_copy(
            src_ref=note_ref.at[peer],
            dst_ref=got_ref.at[me],
            send_sem=sems.at[3],
            recv_sem=sems.at[4],
            device_id={"key": peer},
            device_id_type=MESH,
        ).start()
        return carry

    lax.fori_loop(1, peers, send, 0)
    own.wait()
    own_note.wait()
    others = pl.ds(0, peers - 1)
    for source, target, first in ((packed, out_ref, 1), (note_ref, got_ref, 3)):
        whole = pltpu.make_async_remote_copy(
            src_ref=source.at[others],
            dst_ref=target.at[others],
            send_sem=sems.at[first],
            recv_sem=sems.at[first + 1],
            device_id={"key": peer_at(me, 1)},
            device_id_type=MESH,
        )
        whole.wait_send()
        whole.wait_recv()


def exchange(partials, slot_row, notes, peers):
    rows, feats, days = partials.shape
    return pl.pallas_call(
        functools.partial(exchange_kernel, peers),
        out_shape=(
            jax.ShapeDtypeStruct((peers, feats, days), partials.dtype),
            jax.ShapeDtypeStruct(notes.shape, notes.dtype),
        ),
        in_specs=[
            pl.BlockSpec(memory_space=pl.ANY),
            pl.BlockSpec(memory_space=pltpu.SMEM),
            pl.BlockSpec(memory_space=pltpu.VMEM),
        ],
        out_specs=(pl.BlockSpec(memory_space=pl.ANY), pl.BlockSpec(memory_space=pl.ANY)),
        scratch_shapes=[
            pltpu.VMEM((rows, feats, days), partials.dtype),
            pltpu.VMEM((peers, feats, days), partials.dtype),
            pltpu.SemaphoreType.DMA((6,)),
        ],
        compiler_params=pltpu.CompilerParams(
            collective_id=0, has_side_effects=True, vmem_limit_bytes=32 << 20
        ),
        cost_estimate=pl.CostEstimate(flops=0, bytes_accessed=200_000_000, transcendentals=0),
    )(partials, slot_row, notes)


def window_kernel(
    feats, group, arrived_ref, rate_ref, rows_ref, start_ref, out_ref, square_ref, daily, raw
):
    keys = start_ref.shape[0]
    days_blocks = daily.shape[0]
    step = pl.program_id(0)

    @pl.when(step == 0)
    def _():
        daily[...] = jnp.zeros_like(daily)
        square_ref[...] = jnp.zeros_like(square_ref)

        def add_row(source, carry):
            key = arrived_ref[source]

            @pl.when(key >= 0)
            def _():
                spot = pl.ds(pl.multiple_of(key * feats, feats), feats)
                for b in range(days_blocks):
                    piece = rows_ref[source, :, b * BLOCK : (b + 1) * BLOCK]
                    daily[b, spot, :] += piece.astype(jnp.float32)

            return carry

        lax.fori_loop(0, rows_ref.shape[0], add_row, 0)

    lane = lax.broadcasted_iota(jnp.int32, (keys, BLOCK), 1)
    lag = (
        BLOCK
        + lax.broadcasted_iota(jnp.int32, (2 * BLOCK, BLOCK), 1)
        - lax.broadcasted_iota(jnp.int32, (2 * BLOCK, BLOCK), 0)
    )
    lag_float = lag.astype(jnp.float32)

    def one_feature(local, carry):
        f = step * group + local
        parts = [jnp.zeros((keys, BLOCK), jnp.bfloat16)]
        for b in range(days_blocks):
            piece = daily[b, pl.ds(f, keys, stride=feats), :]
            live = lane + b * BLOCK >= start_ref[...]
            parts.append(jnp.where(live, piece, 0.0).astype(jnp.bfloat16))
        left = jnp.concatenate(
            [jnp.concatenate(parts[b : b + 2], axis=1) for b in range(days_blocks)], axis=0
        )
        bands = []
        for w, length in enumerate(WINDOWS):
            weights = jnp.exp(-rate_ref[w * feats + f] * lag_float)
            inside = (lag >= 0) & (lag < length)
            bands.append(jnp.where(inside, weights, 0.0).astype(jnp.bfloat16))
        result = jnp.dot(left, jnp.concatenate(bands, axis=1), preferred_element_type=jnp.float32)
        for w in range(len(WINDOWS)):
            total = square_ref[w]
            for b in range(days_blocks):
                piece = result[b * keys : (b + 1) * keys, w * BLOCK : (w + 1) * BLOCK]
                raw[w, b, pl.ds(local, keys, stride=group), :] = piece
                total = total + piece * piece
            square_ref[w] = total
        return carry

    lax.fori_loop(0, group, one_feature, 0)

    def pack(key, carry):
        for w in range(len(WINDOWS)):
            for b in range(days_blocks):
                piece = raw[w, b, pl.ds(pl.multiple_of(key * group, group), group), :]
                out_ref[key, w, :, b * BLOCK : (b + 1) * BLOCK] = piece.astype(jnp.bfloat16)
        return carry

    lax.fori_loop(0, keys, pack, 0)


def windows(rows, arrived, active_from, decay_rate):
    sources, feats, days = rows.shape
    keys = active_from.shape[0]
    group = 16
    blocks = days // BLOCK
    kinds = len(WINDOWS)
    start = jnp.broadcast_to(active_from[:, None], (keys, BLOCK))
    return pl.pallas_call(
        functools.partial(window_kernel, feats, group),
        grid=(feats // group,),
        out_shape=(
            jax.ShapeDtypeStruct((keys, kinds, feats, days), jnp.bfloat16),
            jax.ShapeDtypeStruct((kinds, keys, BLOCK), jnp.float32),
        ),
        in_specs=[
            pl.BlockSpec(memory_space=pltpu.SMEM),
            pl.BlockSpec(memory_space=pltpu.SMEM),
            pl.BlockSpec((sources, feats, days), lambda i: (0, 0, 0)),
            pl.BlockSpec((keys, BLOCK), lambda i: (0, 0)),
        ],
        out_specs=(
            pl.BlockSpec((keys, kinds, group, days), lambda i: (0, 0, i, 0)),
            pl.BlockSpec((kinds, keys, BLOCK), lambda i: (0, 0, 0)),
        ),
        scratch_shapes=[
            pltpu.VMEM((blocks, keys * feats, BLOCK), jnp.float32),
            pltpu.VMEM((kinds, blocks, keys * group, BLOCK), jnp.float32),
        ],
        compiler_params=pltpu.CompilerParams(vmem_limit_bytes=56 << 20),
    )(arrived, decay_rate.reshape(-1), rows, start)


def scale_kernel(feats, block, scale_ref, cohort_ref, raw_ref, order_ref, out_ref, table_ref, total, turned):
    step = pl.program_id(0)
    kinds = len(WINDOWS)

    @pl.when(step == 0)
    def _():
        total[...] = jnp.zeros_like(total)

    for local in range(block):
        key = step * block + local
        first = cohort_ref[key] * (kinds * feats)
        for w in range(kinds):
            value = raw_ref[local, w].astype(jnp.float32) * scale_ref[key * kinds + w]
            value = value.astype(jnp.bfloat16)
            out_ref[local, w] = value
            spot = pl.ds(pl.multiple_of(first + w * feats, feats), feats)
            total[spot, :] += value.astype(jnp.float32)

    @pl.when(step == pl.num_programs(0) - 1)
    def _():
        share = order_ref.shape[0] // PLANE
        for g in range(total.shape[0] // BLOCK):
            rows = total[g * BLOCK : (g + 1) * BLOCK, :].astype(jnp.bfloat16)
            by_day = lax.dot_general(
                order_ref[...], rows, (((1,), (1,)), ((), ())), preferred_element_type=jnp.float32
            )
            turned[:, g * share : (g + 1) * share, :] = by_day.reshape(PLANE, share, BLOCK)
        table_ref[...] = turned[...].astype(jnp.bfloat16)


def scale_and_sum(raw, norm_scale, cohort):
    keys, kinds, feats, days = raw.shape
    block = 8
    rows = COHORTS * kinds * feats
    share = days // (NY * NZ * NX)
    place = jnp.arange(days)
    y, x, t, z = place // (days // NY), (place // (share * NZ)) % NX, (place // NZ) % share, place % NZ
    source = ((y * NZ + z) * NX + x) * share + t
    order = (source[:, None] == jnp.arange(days)[None, :]).astype(jnp.bfloat16)
    block_rows = rows // BLOCK * (days // PLANE)
    whole = lambda i: (i, 0, 0, 0)
    return pl.pallas_call(
        functools.partial(scale_kernel, feats, block),
        grid=(keys // block,),
        out_shape=(
            jax.ShapeDtypeStruct(raw.shape, jnp.bfloat16),
            jax.ShapeDtypeStruct((PLANE, block_rows, BLOCK), jnp.bfloat16),
        ),
        in_specs=[
            pl.BlockSpec(memory_space=pltpu.SMEM),
            pl.BlockSpec(memory_space=pltpu.SMEM),
            pl.BlockSpec((block, kinds, feats, days), whole),
            pl.BlockSpec((days, days), lambda i: (0, 0)),
        ],
        out_specs=(
            pl.BlockSpec((block, kinds, feats, days), whole),
            pl.BlockSpec((PLANE, block_rows, BLOCK), lambda i: (0, 0, 0)),
        ),
        scratch_shapes=[
            pltpu.VMEM((rows, days), jnp.float32),
            pltpu.VMEM((PLANE, block_rows, BLOCK), jnp.float32),
        ],
        compiler_params=pltpu.CompilerParams(vmem_limit_bytes=48 << 20),
    )(norm_scale.reshape(-1), cohort, raw, order)


def scatter_kernel(table_ref, out_ref, landed, sums, piece, piece_landed, sems):
    me = lax.axis_index("key")
    y, z, x = me // (NZ * NX), (me // NX) % NZ, me % NX
    barrier = pltpu.get_barrier_semaphore()

    def plane_peer(step):
        ty, tx = (y + step // NX) % NY, (x + step % NX) % NX
        return (ty * NZ + z) * NX + tx, ty * NX + tx

    def line_peer(step):
        tz = (z + step) % NZ
        return (y * NZ + tz) * NX + x, tz

    for step in range(1, PLANE):
        pl.semaphore_signal(barrier, 1, device_id={"key": plane_peer(step)[0]}, device_id_type=MESH)
    for step in range(1, NZ):
        pl.semaphore_signal(barrier, 1, device_id={"key": line_peer(step)[0]}, device_id_type=MESH)
    pl.semaphore_wait(barrier, PLANE - 1 + NZ - 1)

    def send(source, target, step, peer, sem):
        copy = pltpu.make_async_remote_copy(
            src_ref=source,
            dst_ref=target.at[step],
            send_sem=sems.at[0, sem + step],
            recv_sem=sems.at[1, sem + step],
            device_id={"key": peer},
            device_id_type=MESH,
        )
        copy.start()
        return copy

    copies = []
    for step in range(1, PLANE):
        peer, block = plane_peer(step)
        copies.append(send(table_ref.at[block], landed, step, peer, 0))
    for copy in copies:
        copy.wait()
    total = table_ref[y * NX + x].astype(jnp.float32)
    for step in range(1, PLANE):
        total = total + landed[step].astype(jnp.float32)
    sums[...] = total
    count = out_ref.shape[0]
    for tz in range(NZ):
        piece[tz, :count] = sums[pl.ds(tz, count, stride=NZ), :]
    copies = []
    for step in range(1, NZ):
        peer, block = line_peer(step)
        copies.append(send(piece.at[block], piece_landed, step, peer, PLANE))
    for copy in copies:
        copy.wait()
    total = piece[z, :count]
    for step in range(1, NZ):
        total = total + piece_landed[step, :count]
    out_ref[...] = total


def scatter(table):
    _, rows, lanes = table.shape
    own = rows // NZ
    padded = -(-own // 8) * 8
    return pl.pallas_call(
        scatter_kernel,
        out_shape=jax.ShapeDtypeStruct((own, lanes), jnp.float32),
        in_specs=[pl.BlockSpec(memory_space=pltpu.VMEM)],
        out_specs=pl.BlockSpec(memory_space=pltpu.VMEM),
        scratch_shapes=[
            pltpu.VMEM((PLANE, rows, lanes), jnp.bfloat16),
            pltpu.VMEM((rows, lanes), jnp.float32),
            pltpu.VMEM((NZ, padded, lanes), jnp.float32),
            pltpu.VMEM((NZ, padded, lanes), jnp.float32),
            pltpu.SemaphoreType.DMA((2, PLANE + NZ)),
        ],
        compiler_params=pltpu.CompilerParams(
            collective_id=1, has_side_effects=True, vmem_limit_bytes=16 << 20
        ),
    )(table)


def on_device(partials, dest_key, active_from, cohort, decay_rate):
    key_devs = lax.axis_size("key")
    row_count, feat_count, day_count = partials.shape
    key_count = active_from.shape[0]
    kinds = len(WINDOWS)
    match = (dest_key // key_count)[None, :] == jnp.arange(key_devs)[:, None]
    slot_row = jnp.sum(jnp.where(match, jnp.arange(row_count)[None, :], 0), axis=1)
    slot_key = jnp.sum(jnp.where(match, (dest_key % key_count + 1)[None, :], 0), axis=1) - 1
    lane = jnp.arange(BLOCK)
    member = cohort[:, None] == lane[None, :]
    part_count = jnp.sum(member.astype(jnp.int32), axis=0)
    notes = jnp.where(lane[None, :] < COHORTS, part_count[None, :], slot_key[:, None])
    notes = notes.astype(jnp.int32).reshape(key_devs, 1, BLOCK)
    rows, got = exchange(partials, slot_row.astype(jnp.int32), notes, key_devs)
    got = got.reshape(key_devs, BLOCK)
    arrived = got[:, COHORTS]
    whole_count = jnp.sum(got[:, :COHORTS], axis=0).astype(jnp.float32)
    raw, squares = windows(rows, arrived, active_from, decay_rate)
    key_total = lax.psum(jnp.sum(squares, axis=2), "feat")
    norm_scale = lax.rsqrt(key_total.T / (FEAT * day_count) + 1e-05)
    windowed, table = scale_and_sum(raw, norm_scale, cohort)
    own = scatter(table)
    share = day_count // key_devs
    own = own.reshape(-1, share, BLOCK).transpose(0, 2, 1)
    own = own.reshape(COHORTS, kinds, feat_count, share)
    cohort_mean = own / jnp.maximum(whole_count, 1.0)[:, None, None, None]
    return (windowed, cohort_mean)


def solution(mesh):
    placed = (P("key", "feat", None), P("key"), P("key"), P("key"), P(None, "feat"))
    return jax.shard_map(
        on_device,
        mesh=mesh,
        in_specs=placed,
        out_specs=(P("key", None, "feat", None), P(None, None, "feat", "key")),
        check_vma=False,
    )
```

time: 1200 us -> 175 us (0.15)
  blocking collectives: 1040 us -> 2.47 us
  Pallas kernels: 47.9 us -> 160 us
  local copies, waits for them, and re-layouts: 46 us -> 7.58 us
  other arithmetic: 32.4 us -> 3.07 us
  between operations: 15.4 us -> 0.74 us
  matrix products: 13.4 us -> 0 us
    unnamed x1 -> x0, blocking collectives: 696 us -> none
    psum x2 -> x1, blocking collectives: 346 us -> 2.47 us  [on_device(): key_total = lax.psum(jnp.sum(squares, axis=2), 'feat')]
    pallas_call x1 -> x4, Pallas kernels: 47.9 us -> 160 us  [the longest x1 88.3 us: exchange(): pl.pallas_call(functools.partial(exchange_kernel, peers), out_shape=(jax....]
    convert_element_type x4 -> x1, other arithmetic: 27.2 us -> 0.12 us  [scale_and_sum(): order = (source[:, None] == jnp.arange(days)[None, :]).astype(jnp.bfloat16)]
    unnamed x14 -> x7, local copies, waits for them, and re-layouts: 26.4 us -> 3.71 us
    dot_general x3 -> x0, matrix products: 13.4 us -> none  [the longest x1 9.86 us: on_device(): jnp.einsum('kfji,fio->kfjo', pieces, band_weights, preferred_element_type...]
  transfers between devices with their start and end apart: 1 -> 0, of which waited for: 0 -> 0; matrix products, arithmetic and copies ran while one was open for 2% -> 0% of each run, Pallas kernels for 0% -> 0%
where the time goes in v2:
time: 175 us; the launch traced here: 174 us
  Pallas kernels  160 us (91%)
  local copies, waits for them, and re-layouts  7.58 us (4%)
  other arithmetic  3.07 us (2%)
  blocking collectives  2.47 us (1%)
    pallas_call x1, Pallas kernels, exchange(): pl.pallas_call(functools.partial(exchange_kernel, peers), out_shape=(jax....  88.3 us
    pallas_call x1, Pallas kernels, scatter(): pl.pallas_call(scatter_kernel, out_shape=jax.ShapeDtypeStruct((own, lanes...  28.3 us
    pallas_call x1, Pallas kernels, windows(): pl.pallas_call(functools.partial(window_kernel, feats, group), grid=(feat...  28.1 us
    pallas_call x1, Pallas kernels, scale_and_sum(): pl.pallas_call(functools.partial(scale_kernel, feats, block), grid=(keys...  15 us
    unnamed x7, local copies, waits for them, and re-layouts  3.71 us

profile of v2, /device:TPU:2, one launch (start us, length us, event | category | flops | bytes accessed | tf_op | source)
XLA Modules:
  0.0 173.6 jit_solution(5464577594816924354)
XLA Ops:
  0.6 0.0 copy-start.2
  0.6 1.3 reshape.153.rate_ref
  1.9 0.8 convert_reduce_fusion
  2.7 0.7 and_select_fusion.1
  3.4 0.1 select_reduce_fusion
  3.5 0.2 broadcast_select_fusion.note_ref
  3.7 1.4 broadcast_in_dim.66.start_ref
  5.1 0.1 fusion.order_ref
  5.2 0.0 copy-start.1
  5.2 1.4 copy-done.1
  6.6 88.3 %shard_map.68 = (bf16[128,32,384]{2,1,0:T(8,128)(2,1)S(1)}, s32[128,1,128]{2,1,0:T(1,128)S(1)}) custom-call(bf16[64,32,384]{2,1,0:T(8,128)(2,1)S(1)} %copy-done.1, s32[128]{0:T(128)S(1)} %get-tuple-element.21.slot_ref, s32[128,1,128]{2,1,0:T(1,128)S(1)} %broadcast_select_fusion.note_ref), custom_call_target="tpu_custom_call" | custom-call | bytes 200000000 | tf_op jit(solution)/shard_map/pallas_call | solution.py:86
  94.9 0.0 copy-start
  94.9 1.7 copy-done
  96.6 0.8 slice_reduce_fusion.1.arrived_ref
  97.4 28.1 %shard_map.69 = (bf16[128,3,32,384]{3,2,1,0:T(8,128)(2,1)}, f32[3,128,128]{2,1,0:T(8,128)}) custom-call(s32[128]{0:T(128)} %slice_reduce_fusion.1.arrived_ref, f32[96]{0:T(128)} %reshape.153.rate_ref, bf16[128,32,384]{2,1,0:T(8,128)(2,1)} %copy-done, s32[128,128]{1,0:T(8,128)} %broadcast_in_dim.66.start_ref), custom_call_target="tpu_custom_call" | custom-call | tf_op jit(solution)/shard_map/pallas_call | solution.py:188
  125.5 1.1 reduce_sum.48
  126.5 2.5 %psum.7 = f32[3,128]{1,0:T(4,128)S(1)} all-reduce(f32[3,128]{1,0:T(4,128)S(1)} %reduce_sum.48), channel_id=1, replica_groups=mesh['key'=128,'feat'=2] {'feat'}, use_global_device_ids=true, to_apply=%region_4.5 | all-reduce | flops 384 | bytes 3072 | tf_op jit(solution)/shard_map/psum | solution.py:375
  129.0 0.1 copy.12
  129.1 0.2 reshape.154.scale_ref
  129.3 0.0 copy-done.2
  129.4 15.0 %shard_map.70 = (bf16[128,3,32,384]{3,2,1,0:T(8,128)(2,1)}, bf16[16,288,128]{2,1,0:T(8,128)(2,1)S(1)}) custom-call(f32[384]{0:T(512)S(1)} %reshape.154.scale_ref, s32[128]{0:T(128)S(1)} %copy-done.2, bf16[128,3,32,384]{3,2,1,0:T(8,128)(2,1)} %get-tuple-element.11.raw_ref, bf16[384,384]{1,0:T(8,128)(2,1)S(1)} %fusion.order_ref), custom_call_target="tpu_custom_call" | custom-call | tf_op jit(solution)/shard_map/pallas_call | solution.py:254
  144.4 28.3 %shard_map.71 = f32[36,128]{1,0:T(8,128)S(1)} custom-call(bf16[16,288,128]{2,1,0:T(8,128)(2,1)S(1)} %get-tuple-element.13.table_ref), custom_call_target="tpu_custom_call" | custom-call | tf_op jit(solution)/shard_map/pallas_call | solution.py:339
  172.7 0.1 reshape.156
  172.8 0.1 broadcast_divide_fusion
  172.9 0.6 copy.14
  (8 shorter events, 0.1 us)
Async XLA Ops:
  0.6 128.7 %copy-start.2 = (s32[128]{0:T(128)S(1)}, s32[128]{0:T(128)}, u32[]{:S(2)}) copy-start(s32[128]{0:T(128)} %cohort_ref.1) | copy-start | bytes 1540
  5.2 1.4 copy-start.1
  94.9 1.7 copy-start

commit v3 on v0

v3 whole, which is shorter than its diff:
```python
import functools

import jax
import jax.numpy as jnp
from jax import lax
from jax.experimental import pallas as pl
from jax.experimental.pallas import tpu as pltpu
from jax.sharding import PartitionSpec as P

FEAT = 64
BLOCK = 128
WINDOWS = (7, 28, 91)
COHORTS = 16
NY, NZ, NX = 4, 8, 4
PLANE = NY * NX
MESH = pl.DeviceIdType.MESH


DAY_PARTS = 3


def peer_at(me, step):
    y, z, x = me // (NZ * NX), (me // NX) % NZ, me % NX
    dy, dz, dx = step // (NZ * NX), (step // NX) % NZ, step % NX
    return ((y + dy) % NY) * (NZ * NX) + ((z + dz) % NZ) * NX + (x + dx) % NX


def send_to(source, target, send_sem, recv_sem, where):
    copy = pltpu.make_async_remote_copy(
        src_ref=source,
        dst_ref=target,
        send_sem=send_sem,
        recv_sem=recv_sem,
        device_id=where,
        device_id_type=MESH,
    )
    copy.start()
    return copy


def main_kernel(
    slot_ref,
    rate_ref,
    rows_ref,
    note_ref,
    start_ref,
    cohort_ref,
    order_ref,
    raw_ref,
    norm_ref,
    mean_ref,
    held,
    packed,
    landed,
    note_landed,
    wide,
    bands,
    before,
    kept,
    spread,
    staged,
    squares,
    share_out,
    share_in,
    table,
    turned,
    block_out,
    block_in,
    sums,
    piece_out,
    piece_in,
    load_sem,
    send_sems,
    recv_sems,
    pair_sems,
    out_sems,
    block_sems,
    piece_sems,
):
    me = lax.axis_index("key")
    other = {"feat": 1 - lax.axis_index("feat")}
    y, z, x = me // (NZ * NX), (me // NX) % NZ, me % NX
    peers, feats, _ = landed.shape[1:]
    keys = start_ref.shape[1]
    kinds = len(WINDOWS)
    load = pltpu.make_async_copy(rows_ref, held, load_sem)
    load.start()
    barrier = pltpu.get_barrier_semaphore()

    def greet(step, carry):
        pl.semaphore_signal(barrier, 1, device_id={"key": peer_at(me, step)}, device_id_type=MESH)
        return carry

    lax.fori_loop(1, peers, greet, 0)
    pl.semaphore_signal(barrier, 1, device_id=other, device_id_type=MESH)
    load.wait()
    pl.semaphore_wait(barrier, peers)

    for part in range(DAY_PARTS):
        days = slice(part * BLOCK, (part + 1) * BLOCK)

        def send(step, carry):
            peer = peer_at(me, step)
            packed[part, step] = held[slot_ref[peer], :, days]
            where = {"key": peer}
            send_to(packed.at[part, step], landed.at[part, me], send_sems.at[part], recv_sems.at[part], where)
            if part == 0:
                send_to(note_ref.at[peer], note_landed.at[me], send_sems.at[DAY_PARTS], recv_sems.at[DAY_PARTS], where)
            return carry

        lax.fori_loop(1, peers, send, 0)
        landed[part, me] = held[slot_ref[me], :, days]
    note_landed[me] = note_ref[me]

    shape = (2 * BLOCK, BLOCK)
    lag = BLOCK + lax.broadcasted_iota(jnp.int32, shape, 1) - lax.broadcasted_iota(jnp.int32, shape, 0)
    lag_float = lag.astype(jnp.float32)

    def make_band(f, carry):
        for w, length in enumerate(WINDOWS):
            weights = jnp.exp(-rate_ref[w, f] * lag_float)
            inside = (lag >= 0) & (lag < length)
            band = jnp.where(inside, weights, 0.0).astype(jnp.bfloat16)
            bands[f, :, w * BLOCK : (w + 1) * BLOCK] = band
        return carry

    lax.fori_loop(0, feats, make_band, 0)

    start = jnp.broadcast_to(start_ref[...].astype(jnp.float32), (keys, BLOCK)).T
    lane = lax.broadcasted_iota(jnp.int32, (keys, BLOCK), 1)
    lane_float = lane.astype(jnp.float32)
    squares[...] = jnp.zeros_like(squares)

    def whole(source, target, index):
        others = pl.ds(0, peers - 1)
        return pltpu.make_async_remote_copy(
            src_ref=source.at[others],
            dst_ref=target.at[others],
            send_sem=send_sems.at[index],
            recv_sem=recv_sems.at[index],
            device_id={"key": peer_at(me, 1)},
            device_id_type=MESH,
        )

    notes = whole(note_ref, note_landed, DAY_PARTS)
    notes.wait_recv()
    arrived = note_landed[:, 0, :BLOCK]
    receive = jnp.where(arrived == lane, 1.0, 0.0).T.astype(jnp.bfloat16)
    count = jnp.sum(note_landed[:, 0, BLOCK:], axis=0, keepdims=True).astype(jnp.float32)

    def pack(part):
        def one_key(key, carry):
            spot = pl.ds(pl.multiple_of(key * feats, feats), feats)
            for w in range(kinds):
                staged[part % 2, key, w] = spread[w, spot, :].astype(jnp.bfloat16)
            return carry

        lax.fori_loop(0, keys, one_key, 0)
        copy = pltpu.make_async_copy(
            staged.at[part % 2],
            raw_ref.at[:, :, :, pl.ds(part * BLOCK, BLOCK)],
            out_sems.at[part],
        )
        copy.start()
        return copy

    writes = []
    for part in range(DAY_PARTS):
        arrival = whole(packed.at[part], landed.at[part], part)
        arrival.wait_recv()

        def widen(source, carry):
            spot = pl.ds(pl.multiple_of(source * feats, feats), feats)
            wide[spot, :] = landed[part, source].astype(jnp.float32)
            return carry

        lax.fori_loop(0, peers, widen, 0)
        live = lane_float + float(part * BLOCK) >= start

        def features(pair, carry):
            columns = []
            for local in range(2):
                f = pair * 2 + local
                columns.append(wide[pl.ds(f, peers, stride=feats), :].astype(jnp.bfloat16))
            summed = jnp.dot(receive, jnp.concatenate(columns, axis=1), preferred_element_type=jnp.float32)
            for local in range(2):
                f = pair * 2 + local
                daily = summed[:, local * BLOCK : (local + 1) * BLOCK]
                daily = jnp.where(live, daily, 0.0).astype(jnp.bfloat16)
                if part == 0:
                    result = jnp.dot(daily, bands[f, BLOCK:, :], preferred_element_type=jnp.float32)
                else:
                    both = jnp.concatenate([before[f], daily], axis=1)
                    result = jnp.dot(both, bands[f], preferred_element_type=jnp.float32)
                if part < DAY_PARTS - 1:
                    before[f] = daily
                kept[f, part] = result.astype(jnp.bfloat16)
                for w in range(kinds):
                    piece = result[:, w * BLOCK : (w + 1) * BLOCK]
                    spread[w, pl.ds(f, keys, stride=feats), :] = piece
                    squares[w] += piece * piece
            return carry

        lax.fori_loop(0, feats // 2, features, 0)
        if part < DAY_PARTS - 1:
            writes.append(pack(part))

    for w in range(kinds):
        share_out[w : w + 1, :] = jnp.sum(squares[w].T, axis=0, keepdims=True)
    share = send_to(share_out, share_in, pair_sems.at[0], pair_sems.at[1], other)
    share.wait()
    mean_square = (share_out[...] + share_in[...]) / (FEAT * DAY_PARTS * BLOCK)
    norm = lax.rsqrt(mean_square + 1e-05)
    norm_ref[...] = norm
    cohort_row = lax.broadcasted_iota(jnp.int32, (COHORTS, keys), 0)
    member = cohort_row == jnp.broadcast_to(cohort_ref[...], (COHORTS, keys))
    weights = [jnp.where(member, norm[w : w + 1, :], 0.0) for w in range(kinds)]
    weights = jnp.concatenate(weights, axis=0)
    high = weights.astype(jnp.bfloat16)
    low = (weights - high.astype(jnp.float32)).astype(jnp.bfloat16)
    weights = jnp.concatenate([high, low], axis=0)

    def add_cohorts(f, carry):
        for part in range(DAY_PARTS):
            result = jnp.dot(weights, kept[f, part], preferred_element_type=jnp.float32)
            for w in range(kinds):
                lanes = slice(w * BLOCK, (w + 1) * BLOCK)
                top = result[w * COHORTS : (w + 1) * COHORTS, lanes]
                rest = result[(kinds + w) * COHORTS : (kinds + w + 1) * COHORTS, lanes]
                spot = pl.ds(pl.multiple_of(f * COHORTS, COHORTS), COHORTS)
                table[w, spot, part * BLOCK : (part + 1) * BLOCK] = top + rest
        return carry

    lax.fori_loop(0, feats, add_cohorts, 0)

    def plane_peer(step):
        ty, tx = (y + step // NX) % NY, (x + step % NX) % NX
        return (ty * NZ + z) * NX + tx, ty * NX + tx

    def line_peer(step):
        tz = (z + step) % NZ
        return (y * NZ + tz) * NX + x, tz

    rows = block_out.shape[2]
    each = order_ref.shape[0] // PLANE
    block_copies = []
    for w in range(kinds):
        for g in range(rows // each):
            lines = table[w, g * BLOCK : (g + 1) * BLOCK, :].astype(jnp.bfloat16)
            by_day = lax.dot_general(
                order_ref[...], lines, (((1,), (1,)), ((), ())), preferred_element_type=jnp.float32
            )
            turned[:, g * each : (g + 1) * each, :] = by_day.reshape(PLANE, each, BLOCK)
        block_out[w] = turned[...].astype(jnp.bfloat16)
        for step in range(1, PLANE):
            peer, block = plane_peer(step)
            sems = block_sems.at[0, w, step], block_sems.at[1, w, step]
            block_copies.append(
                send_to(block_out.at[w, block], block_in.at[w, step], *sems, {"key": peer})
            )
    writes[0].wait()
    last_write = pack(DAY_PARTS - 1)
    for w in range(kinds):
        total = block_out[w, y * NX + x].astype(jnp.float32)
        for step in range(1, PLANE):
            block_copies[w * (PLANE - 1) + step - 1].wait_recv()
            total = total + block_in[w, step].astype(jnp.float32)
        sums[w * rows : (w + 1) * rows, :] = total
    own_rows = mean_ref.shape[0]
    for tz in range(NZ):
        piece_out[tz, :own_rows] = sums[pl.ds(tz, own_rows, stride=NZ), :]
    piece_copies = []
    for step in range(1, NZ):
        peer, block = line_peer(step)
        sems = piece_sems.at[0, step], piece_sems.at[1, step]
        piece_copies.append(send_to(piece_out.at[block], piece_in.at[step], *sems, {"key": peer}))
    total = piece_out[z, :own_rows]
    for step in range(1, NZ):
        piece_copies[step - 1].wait_recv()
        total = total + piece_in[step, :own_rows]
    mean_ref[...] = total / jnp.maximum(count, 1.0)

    for part in range(DAY_PARTS):
        whole(packed.at[part], landed.at[part], part).wait_send()
    notes.wait_send()
    for copy in block_copies + piece_copies:
        copy.wait_send()
    writes[1].wait()
    last_write.wait()


def day_order(days):
    share = days // (NY * NZ * NX)
    place = jnp.arange(days)
    y, x, t, z = place // (days // NY), (place // (share * NZ)) % NX, (place // NZ) % share, place % NZ
    source = ((y * NZ + z) * NX + x) * share + t
    return (source[:, None] == jnp.arange(days)[None, :]).astype(jnp.bfloat16)


def main(partials, slot_row, notes, active_from, cohort, decay_rate):
    rows, feats, days = partials.shape
    peers = slot_row.shape[0]
    keys = active_from.shape[0]
    kinds = len(WINDOWS)
    lines = feats * COHORTS
    block_rows = lines // BLOCK * (days // PLANE)
    own_rows = kinds * block_rows // NZ
    padded = -(-own_rows // 8) * 8
    vmem = pl.BlockSpec(memory_space=pltpu.VMEM)
    smem = pl.BlockSpec(memory_space=pltpu.SMEM)
    hbm = pl.BlockSpec(memory_space=pl.ANY)
    half, full = jnp.bfloat16, jnp.float32
    return pl.pallas_call(
        main_kernel,
        out_shape=(
            jax.ShapeDtypeStruct((keys, kinds, feats, days), half),
            jax.ShapeDtypeStruct((kinds, keys), full),
            jax.ShapeDtypeStruct((own_rows, BLOCK), full),
        ),
        in_specs=[smem, smem, hbm, vmem, vmem, vmem, vmem],
        out_specs=(hbm, vmem, vmem),
        scratch_shapes=[
            pltpu.VMEM((rows, feats, days), half),
            pltpu.VMEM((DAY_PARTS, peers, feats, BLOCK), half),
            pltpu.VMEM((DAY_PARTS, peers, feats, BLOCK), half),
            pltpu.VMEM(notes.shape, notes.dtype),
            pltpu.VMEM((peers * feats, BLOCK), full),
            pltpu.VMEM((feats, 2 * BLOCK, kinds * BLOCK), half),
            pltpu.VMEM((feats, keys, BLOCK), half),
            pltpu.VMEM((feats, DAY_PARTS, keys, kinds * BLOCK), half),
            pltpu.VMEM((kinds, keys * feats, BLOCK), full),
            pltpu.VMEM((2, keys, kinds, feats, BLOCK), half),
            pltpu.VMEM((kinds, keys, BLOCK), full),
            pltpu.VMEM((kinds, keys), full),
            pltpu.VMEM((kinds, keys), full),
            pltpu.VMEM((kinds, lines, days), full),
            pltpu.VMEM((PLANE, block_rows, BLOCK), full),
            pltpu.VMEM((kinds, PLANE, block_rows, BLOCK), half),
            pltpu.VMEM((kinds, PLANE, block_rows, BLOCK), half),
            pltpu.VMEM((kinds * block_rows, BLOCK), full),
            pltpu.VMEM((NZ, padded, BLOCK), full),
            pltpu.VMEM((NZ, padded, BLOCK), full),
            pltpu.SemaphoreType.DMA,
            pltpu.SemaphoreType.DMA((DAY_PARTS + 1,)),
            pltpu.SemaphoreType.DMA((DAY_PARTS + 1,)),
            pltpu.SemaphoreType.DMA((2,)),
            pltpu.SemaphoreType.DMA((DAY_PARTS,)),
            pltpu.SemaphoreType.DMA((2, kinds, PLANE)),
            pltpu.SemaphoreType.DMA((2, NZ)),
        ],
        compiler_params=pltpu.CompilerParams(
            collective_id=0, has_side_effects=True, vmem_limit_bytes=60 << 20
        ),
    )(
        slot_row,
        decay_rate,
        partials,
        notes,
        active_from.reshape(1, keys),
        cohort.reshape(1, keys),
        day_order(days),
    )


def scale_kernel(scale_ref, raw_ref, out_ref):
    block, kinds = raw_ref.shape[:2]
    step = pl.program_id(0)
    for local in range(block):
        for w in range(kinds):
            value = raw_ref[local, w].astype(jnp.float32) * scale_ref[w, step * block + local]
            out_ref[local, w] = value.astype(jnp.bfloat16)


def scale(raw, norm_scale):
    keys, kinds, feats, days = raw.shape
    block = 16
    spec = pl.BlockSpec((block, kinds, feats, days), lambda i: (i, 0, 0, 0))
    return pl.pallas_call(
        scale_kernel,
        grid=(keys // block,),
        out_shape=jax.ShapeDtypeStruct(raw.shape, jnp.bfloat16),
        in_specs=[pl.BlockSpec(memory_space=pltpu.SMEM), spec],
        out_specs=spec,
        compiler_params=pltpu.CompilerParams(vmem_limit_bytes=60 << 20),
    )(norm_scale, raw)


def on_device(partials, dest_key, active_from, cohort, decay_rate):
    key_devs = lax.axis_size("key")
    row_count, feat_count, day_count = partials.shape
    key_count = active_from.shape[0]
    match = (dest_key // key_count)[None, :] == jnp.arange(key_devs)[:, None]
    slot_row = jnp.sum(jnp.where(match, jnp.arange(row_count)[None, :], 0), axis=1)
    slot_key = jnp.sum(jnp.where(match, (dest_key % key_count + 1)[None, :], 0), axis=1) - 1
    lane = jnp.arange(2 * BLOCK)
    member = cohort[:, None] == lane[None, :] % COHORTS
    part_count = jnp.sum(member.astype(jnp.int32), axis=0)
    notes = jnp.where(lane[None, :] < BLOCK, slot_key[:, None], part_count[None, :])
    notes = notes.astype(jnp.int32).reshape(key_devs, 1, 2 * BLOCK)
    slot_row = slot_row.astype(jnp.int32)
    raw, norm_scale, own = main(partials, slot_row, notes, active_from, cohort, decay_rate)
    windowed = scale(raw, norm_scale)
    kinds = len(WINDOWS)
    share = day_count // key_devs
    own = own.reshape(kinds, feat_count * COHORTS // BLOCK, share, BLOCK // COHORTS, COHORTS)
    own = own.transpose(4, 0, 1, 3, 2)
    return (windowed, own.reshape(COHORTS, kinds, feat_count, share))


def solution(mesh):
    placed = (P("key", "feat", None), P("key"), P("key"), P("key"), P(None, "feat"))
    return jax.shard_map(
        on_device,
        mesh=mesh,
        in_specs=placed,
        out_specs=(P("key", None, "feat", None), P(None, None, "feat", "key")),
        check_vma=False,
    )
```

time: 589 us -> 152 us (0.26)
  blocking collectives: 351 us -> 0 us
  Pallas kernels: 0 us -> 146 us
  waiting for transfers between devices: 72.9 us -> 0 us
  other arithmetic: 63.2 us -> 3.75 us
  local copies, waits for them, and re-layouts: 38.9 us -> 0.85 us
  starting transfers between devices: 23.9 us -> 0 us
  matrix products: 21.7 us -> 0 us
  between operations: 14.2 us -> 0.68 us
    psum x2 -> x0, blocking collectives: 351 us -> none  [the longest x1 349 us: on_device(): whole_table, whole_count = lax.psum((part_table, part_count), 'key')]
    pallas_call x0 -> x2, Pallas kernels: none -> 146 us  [the longest x1 136 us: main(): pl.pallas_call(main_kernel, out_shape=(jax.ShapeDtypeStruct((keys, kinds,...]
    all_to_all x2 -> x0, waiting for transfers between devices: 72.9 us -> none  [the longest x1 67.2 us: on_device(): lax.all_to_all(packed, 'key', split_axis=0, concat_axis=0, tiled=True)]
    convert_element_type x5 -> x1, other arithmetic: 54.7 us -> 0.83 us  [day_order(): return (source[:, None] == jnp.arange(days)[None, :]).astype(jnp.bfloat16)]
    all_to_all x2 -> x0, starting transfers between devices: 23.7 us -> none  [the longest x1 15.4 us: on_device(): lax.all_to_all(slot_local, 'key', split_axis=0, concat_axis=0, tiled=True)]
    dot_general x4 -> x0, matrix products: 21.7 us -> none  [the longest x1 9.85 us: on_device(): jnp.einsum('kfji,fio->kfjo', pieces, band_weights, preferred_element_type...]
    unnamed x16 -> x3, local copies, waits for them, and re-layouts: 19.2 us -> 0.74 us
    convert_element_type x1 -> x0, local copies, waits for them, and re-layouts: 12.8 us -> none  [on_device(): raw_float = raw_window.astype(jnp.float32)]
  transfers between devices with their start and end apart: 3 -> 0, of which waited for: 2 -> 0; matrix products, arithmetic and copies ran while one was open for 6% -> 0% of each run, Pallas kernels for 0% -> 0%
where the time goes in v3:
time: 152 us; the launch traced here: 151 us
  Pallas kernels  146 us (96%)
  other arithmetic  3.75 us (2%)
    pallas_call x1, Pallas kernels, main(): pl.pallas_call(main_kernel, out_shape=(jax.ShapeDtypeStruct((keys, kinds,...  136 us
    pallas_call x1, Pallas kernels, scale(): pl.pallas_call(scale_kernel, grid=(keys // block,), out_shape=jax.ShapeDt...  10.1 us

profile of v3, /device:TPU:2, one launch (start us, length us, event | category | flops | bytes accessed | tf_op | source)
XLA Modules:
  0.0 151.2 jit_solution(10316398267244362810)
XLA Ops:
  0.7 0.8 convert_reduce_fusion
  1.4 0.7 and_select_fusion.2
  2.1 0.6 select_reduce_fusion
  2.7 0.9 broadcast_select_fusion.note_ref
  3.6 0.8 fusion.order_ref
  4.4 135.8 %shard_map.68 = (bf16[128,3,32,384]{3,2,1,0:T(8,128)(2,1)}, f32[3,128]{1,0:T(4,128)}, f32[36,128]{1,0:T(8,128)}) custom-call(s32[128]{0:T(128)} %get-tuple-element.13.slot_ref, f32[3,32]{1,0:T(4,128)} %rate_ref.1, bf16[64,32,384]{2,1,0:T(8,128)(2,1)} %rows_ref.1, s32[128,1,256]{2,1,0:T(1,128)} %broadcast_select_fusion.note_ref, s32[1,128]{1,0:T(1,128)} %bitcast.9, ...), custom_call_target="tpu_custom_call" | custom-call | tf_op jit(solution)/shard_map/pallas_call | solution.py:313
  140.2 0.0 copy-start
  140.2 10.1 %shard_map.69 = bf16[128,3,32,384]{3,2,1,0:T(8,128)(2,1)} custom-call(f32[3,128]{1,0:T(4,128)} %get-tuple-element.5.scale_ref, bf16[128,3,32,384]{3,2,1,0:T(8,128)(2,1)} %get-tuple-element.6.raw_ref), custom_call_target="tpu_custom_call" | custom-call | tf_op jit(solution)/shard_map/pallas_call | solution.py:378
  150.3 0.0 copy-done
  150.3 0.1 reshape.161
  150.4 0.7 copy.11
  (5 shorter events, 0.0 us)
Async XLA Ops:
  140.2 10.1 %copy-start = (f32[36,128]{1,0:T(8,128)S(1)}, f32[36,128]{1,0:T(8,128)}, u32[]{:S(2)}) copy-start(f32[36,128]{1,0:T(8,128)} %get-tuple-element.7) | copy-start | bytes 55300

commit v4 on v3

--- a/solution.py
+++ b/solution.py
@@ -2,6 +2,7 @@
 
 import jax
 import jax.numpy as jnp
+import numpy as np
 from jax import lax
 from jax.experimental import pallas as pl
 from jax.experimental.pallas import tpu as pltpu
@@ -17,12 +18,21 @@
 
 
 DAY_PARTS = 3
+AT_ONCE = 4
 
 
 def peer_at(me, step):
     y, z, x = me // (NZ * NX), (me // NX) % NZ, me % NX
     dy, dz, dx = step // (NZ * NX), (step // NX) % NZ, step % NX
     return ((y + dy) % NY) * (NZ * NX) + ((z + dz) % NZ) * NX + (x + dx) % NX
+
+
+def far_first(peers):
+    def distance(step):
+        place = (step // (NZ * NX), NY), ((step // NX) % NZ, NZ), (step % NX, NX)
+        return sum(min(d, n - d) for d, n in place)
+
+    return sorted(range(1, peers), key=lambda step: (-distance(step), step))
 
 
 def send_to(source, target, send_sem, recv_sem, where):
@@ -39,10 +49,9 @@
 
 
 def main_kernel(
-    slot_ref,
     rate_ref,
     rows_ref,
-    note_ref,
+    dest_ref,
     start_ref,
     cohort_ref,
     order_ref,
@@ -50,6 +59,9 @@
     norm_ref,
     mean_ref,
     held,
+    slot_row,
+    slot_ref,
+    note_ref,
     packed,
     landed,
     note_landed,
@@ -87,12 +99,29 @@
     load.start()
     barrier = pltpu.get_barrier_semaphore()
 
-    def greet(step, carry):
+    for step in far_first(peers):
         pl.semaphore_signal(barrier, 1, device_id={"key": peer_at(me, step)}, device_id_type=MESH)
-        return carry
-
-    lax.fori_loop(1, peers, greet, 0)
     pl.semaphore_signal(barrier, 1, device_id=other, device_id_type=MESH)
+
+    row_count = held.shape[0]
+    square = (peers, BLOCK)
+    sub = lax.broadcasted_iota(jnp.int32, square, 0)
+    lane = lax.broadcasted_iota(jnp.int32, square, 1)
+
+    def down(row):
+        return jnp.broadcast_to(row, square).T
+
+    dest = jnp.broadcast_to(dest_ref[...], (peers, row_count)).T
+    match = dest // keys == lane[:row_count]
+    slot_row[...] = jnp.max(jnp.where(match, sub[:row_count], 0), axis=0, keepdims=True)
+    to_scalar = pltpu.make_async_copy(slot_row, slot_ref, pair_sems.at[0])
+    to_scalar.start()
+    slot_key = jnp.max(jnp.where(match, dest % keys, -1), axis=0, keepdims=True)
+    note_ref[:, 0, :BLOCK] = down(slot_key)
+    in_cohort = down(cohort_ref[...]) == lane % COHORTS
+    part_count = jnp.sum(jnp.where(in_cohort, 1, 0), axis=0, keepdims=True)
+    note_ref[:, 0, BLOCK:] = jnp.broadcast_to(part_count, square)
+    to_scalar.wait()
     load.wait()
     pl.semaphore_wait(barrier, peers)
 
@@ -101,7 +130,7 @@
 
         def send(step, carry):
             peer = peer_at(me, step)
-            packed[part, step] = held[slot_ref[peer], :, days]
+            packed[part, step] = held[slot_ref[0, peer], :, days]
             where = {"key": peer}
             send_to(packed.at[part, step], landed.at[part, me], send_sems.at[part], recv_sems.at[part], where)
             if part == 0:
@@ -109,7 +138,7 @@
             return carry
 
         lax.fori_loop(1, peers, send, 0)
-        landed[part, me] = held[slot_ref[me], :, days]
+        landed[part, me] = held[slot_ref[0, me], :, days]
     note_landed[me] = note_ref[me]
 
     shape = (2 * BLOCK, BLOCK)
@@ -126,9 +155,7 @@
 
     lax.fori_loop(0, feats, make_band, 0)
 
-    start = jnp.broadcast_to(start_ref[...].astype(jnp.float32), (keys, BLOCK)).T
-    lane = lax.broadcasted_iota(jnp.int32, (keys, BLOCK), 1)
-    lane_float = lane.astype(jnp.float32)
+    start = down(start_ref[...])
     squares[...] = jnp.zeros_like(squares)
 
     def whole(source, target, index):
@@ -149,13 +176,22 @@
     count = jnp.sum(note_landed[:, 0, BLOCK:], axis=0, keepdims=True).astype(jnp.float32)
 
     def pack(part):
-        def one_key(key, carry):
-            spot = pl.ds(pl.multiple_of(key * feats, feats), feats)
+        def interleave(f, carry):
             for w in range(kinds):
-                staged[part % 2, key, w] = spread[w, spot, :].astype(jnp.bfloat16)
+                piece = kept[f, part, :, w * BLOCK : (w + 1) * BLOCK].astype(jnp.float32)
+                spread[w, pl.ds(f, keys, stride=feats), :] = piece
             return carry
 
-        lax.fori_loop(0, keys, one_key, 0)
+        lax.fori_loop(0, feats, interleave, 0, unroll=2)
+
+        def some_keys(some, carry):
+            for w in range(kinds):
+                spot = pl.ds(pl.multiple_of(some * 4 * feats, 4 * feats), 4 * feats)
+                piece = spread[w, spot, :].astype(jnp.bfloat16)
+                staged[part % 2, pl.ds(some * 4, 4), w] = piece.reshape(4, feats, BLOCK)
+            return carry
+
+        lax.fori_loop(0, keys // 4, some_keys, 0)
         copy = pltpu.make_async_copy(
             staged.at[part % 2],
             raw_ref.at[:, :, :, pl.ds(part * BLOCK, BLOCK)],
@@ -169,22 +205,24 @@
         arrival = whole(packed.at[part], landed.at[part], part)
         arrival.wait_recv()
 
-        def widen(source, carry):
-            spot = pl.ds(pl.multiple_of(source * feats, feats), feats)
-            wide[spot, :] = landed[part, source].astype(jnp.float32)
+        def widen(some, carry):
+            spot = pl.ds(pl.multiple_of(some * 8 * feats, 8 * feats), 8 * feats)
+            piece = landed[part, pl.ds(some * 8, 8)].astype(jnp.float32)
+            wide[spot, :] = piece.reshape(8 * feats, BLOCK)
             return carry
 
-        lax.fori_loop(0, peers, widen, 0)
-        live = lane_float + float(part * BLOCK) >= start
-
-        def features(pair, carry):
+        lax.fori_loop(0, peers // 8, widen, 0)
+        live = lane + part * BLOCK >= start
+
+        def features(group, carry):
             columns = []
-            for local in range(2):
-                f = pair * 2 + local
+            for local in range(AT_ONCE):
+                f = group * AT_ONCE + local
                 columns.append(wide[pl.ds(f, peers, stride=feats), :].astype(jnp.bfloat16))
             summed = jnp.dot(receive, jnp.concatenate(columns, axis=1), preferred_element_type=jnp.float32)
-            for local in range(2):
-                f = pair * 2 + local
+            results = []
+            for local in range(AT_ONCE):
+                f = group * AT_ONCE + local
                 daily = summed[:, local * BLOCK : (local + 1) * BLOCK]
                 daily = jnp.where(live, daily, 0.0).astype(jnp.bfloat16)
                 if part == 0:
@@ -195,13 +233,13 @@
                 if part < DAY_PARTS - 1:
                     before[f] = daily
                 kept[f, part] = result.astype(jnp.bfloat16)
-                for w in range(kinds):
-                    piece = result[:, w * BLOCK : (w + 1) * BLOCK]
-                    spread[w, pl.ds(f, keys, stride=feats), :] = piece
-                    squares[w] += piece * piece
+                results.append(result)
+            for w in range(kinds):
+                pieces = [result[:, w * BLOCK : (w + 1) * BLOCK] for result in results]
+                squares[w] += sum(piece * piece for piece in pieces)
             return carry
 
-        lax.fori_loop(0, feats // 2, features, 0)
+        lax.fori_loop(0, feats // AT_ONCE, features, 0)
         if part < DAY_PARTS - 1:
             writes.append(pack(part))
 
@@ -214,24 +252,26 @@
     norm_ref[...] = norm
     cohort_row = lax.broadcasted_iota(jnp.int32, (COHORTS, keys), 0)
     member = cohort_row == jnp.broadcast_to(cohort_ref[...], (COHORTS, keys))
-    weights = [jnp.where(member, norm[w : w + 1, :], 0.0) for w in range(kinds)]
-    weights = jnp.concatenate(weights, axis=0)
-    high = weights.astype(jnp.bfloat16)
-    low = (weights - high.astype(jnp.float32)).astype(jnp.bfloat16)
-    weights = jnp.concatenate([high, low], axis=0)
-
-    def add_cohorts(f, carry):
-        for part in range(DAY_PARTS):
-            result = jnp.dot(weights, kept[f, part], preferred_element_type=jnp.float32)
-            for w in range(kinds):
-                lanes = slice(w * BLOCK, (w + 1) * BLOCK)
-                top = result[w * COHORTS : (w + 1) * COHORTS, lanes]
-                rest = result[(kinds + w) * COHORTS : (kinds + w + 1) * COHORTS, lanes]
-                spot = pl.ds(pl.multiple_of(f * COHORTS, COHORTS), COHORTS)
-                table[w, spot, part * BLOCK : (part + 1) * BLOCK] = top + rest
+    weights = []
+    for w in range(kinds):
+        scaled = jnp.where(member, norm[w : w + 1, :], 0.0)
+        high = scaled.astype(jnp.bfloat16)
+        low = (scaled - high.astype(jnp.float32)).astype(jnp.bfloat16)
+        weights.append(jnp.concatenate([high, low], axis=0))
+
+    def add_cohorts(group, carry):
+        for local in range(AT_ONCE):
+            f = group * AT_ONCE + local
+            spot = pl.ds(pl.multiple_of(f * COHORTS, COHORTS), COHORTS)
+            for part in range(DAY_PARTS):
+                for w in range(kinds):
+                    lanes = slice(w * BLOCK, (w + 1) * BLOCK)
+                    result = jnp.dot(weights[w], kept[f, part, :, lanes], preferred_element_type=jnp.float32)
+                    both = result[:COHORTS] + result[COHORTS:]
+                    table[w, spot, part * BLOCK : (part + 1) * BLOCK] = both
         return carry
 
-    lax.fori_loop(0, feats, add_cohorts, 0)
+    lax.fori_loop(0, feats // AT_ONCE, add_cohorts, 0)
 
     def plane_peer(step):
         ty, tx = (y + step // NX) % NY, (x + step % NX) % NX
@@ -291,15 +331,14 @@
 
 def day_order(days):
     share = days // (NY * NZ * NX)
-    place = jnp.arange(days)
+    place = np.arange(days)
     y, x, t, z = place // (days // NY), (place // (share * NZ)) % NX, (place // NZ) % share, place % NZ
     source = ((y * NZ + z) * NX + x) * share + t
-    return (source[:, None] == jnp.arange(days)[None, :]).astype(jnp.bfloat16)
-
-
-def main(partials, slot_row, notes, active_from, cohort, decay_rate):
+    return jnp.asarray(source[:, None] == place[None, :], jnp.bfloat16)
+
+
+def main(partials, dest_key, active_from, cohort, decay_rate, peers):
     rows, feats, days = partials.shape
-    peers = slot_row.shape[0]
     keys = active_from.shape[0]
     kinds = len(WINDOWS)
     lines = feats * COHORTS
@@ -317,13 +356,16 @@
             jax.ShapeDtypeStruct((kinds, keys), full),
             jax.ShapeDtypeStruct((own_rows, BLOCK), full),
         ),
-        in_specs=[smem, smem, hbm, vmem, vmem, vmem, vmem],
+        in_specs=[smem, hbm, vmem, vmem, vmem, vmem],
         out_specs=(hbm, vmem, vmem),
         scratch_shapes=[
             pltpu.VMEM((rows, feats, days), half),
+            pltpu.VMEM((1, peers), jnp.int32),
+            pltpu.SMEM((1, peers), jnp.int32),
+            pltpu.VMEM((peers, 1, 2 * BLOCK), jnp.int32),
             pltpu.VMEM((DAY_PARTS, peers, feats, BLOCK), half),
             pltpu.VMEM((DAY_PARTS, peers, feats, BLOCK), half),
-            pltpu.VMEM(notes.shape, notes.dtype),
+            pltpu.VMEM((peers, 1, 2 * BLOCK), jnp.int32),
             pltpu.VMEM((peers * feats, BLOCK), full),
             pltpu.VMEM((feats, 2 * BLOCK, kinds * BLOCK), half),
             pltpu.VMEM((feats, keys, BLOCK), half),
@@ -352,10 +394,9 @@
             collective_id=0, has_side_effects=True, vmem_limit_bytes=60 << 20
         ),
     )(
-        slot_row,
         decay_rate,
         partials,
-        notes,
+        dest_key.reshape(1, rows),
         active_from.reshape(1, keys),
         cohort.reshape(1, keys),
         day_order(days),
@@ -387,18 +428,8 @@
 
 def on_device(partials, dest_key, active_from, cohort, decay_rate):
     key_devs = lax.axis_size("key")
-    row_count, feat_count, day_count = partials.shape
-    key_count = active_from.shape[0]
-    match = (dest_key // key_count)[None, :] == jnp.arange(key_devs)[:, None]
-    slot_row = jnp.sum(jnp.where(match, jnp.arange(row_count)[None, :], 0), axis=1)
-    slot_key = jnp.sum(jnp.where(match, (dest_key % key_count + 1)[None, :], 0), axis=1) - 1
-    lane = jnp.arange(2 * BLOCK)
-    member = cohort[:, None] == lane[None, :] % COHORTS
-    part_count = jnp.sum(member.astype(jnp.int32), axis=0)
-    notes = jnp.where(lane[None, :] < BLOCK, slot_key[:, None], part_count[None, :])
-    notes = notes.astype(jnp.int32).reshape(key_devs, 1, 2 * BLOCK)
-    slot_row = slot_row.astype(jnp.int32)
-    raw, norm_scale, own = main(partials, slot_row, notes, active_from, cohort, decay_rate)
+    _, feat_count, day_count = partials.shape
+    raw, norm_scale, own = main(partials, dest_key, active_from, cohort, decay_rate, key_devs)
     windowed = scale(raw, norm_scale)
     kinds = len(WINDOWS)
     share = day_count // key_devs

time: 152 us -> 133 us (0.88)
  Pallas kernels: 146 us -> 130 us
  other arithmetic: 3.75 us -> 0 us
    pallas_call x1, Pallas kernels: 136 us -> 120 us  [main(): pl.pallas_call(main_kernel, out_shape=(jax.ShapeDtypeStruct((keys, kinds,...]
    select_n x3 -> x0, other arithmetic: 1.53 us -> none  [the longest x1 0.85 us: on_device(): jnp.where(lane[None, :] < BLOCK, slot_key[:, None], part_count[None, :])]
where the time goes in v4:
time: 133 us; the launch traced here: 132 us
  Pallas kernels  130 us (98%)
    pallas_call x1, Pallas kernels, main(): pl.pallas_call(main_kernel, out_shape=(jax.ShapeDtypeStruct((keys, kinds,...  120 us
    pallas_call x1, Pallas kernels, scale(): pl.pallas_call(scale_kernel, grid=(keys // block,), out_shape=jax.ShapeDt...  10.1 us

profile of v4, /device:TPU:2, one launch (start us, length us, event | category | flops | bytes accessed | tf_op | source)
XLA Modules:
  0.0 131.5 jit_solution(14705728682767836700)
XLA Ops:
  0.6 120.0 %shard_map.77 = (bf16[128,3,32,384]{3,2,1,0:T(8,128)(2,1)}, f32[3,128]{1,0:T(4,128)}, f32[36,128]{1,0:T(8,128)}) custom-call(f32[3,32]{1,0:T(4,128)} %rate_ref.1, bf16[64,32,384]{2,1,0:T(8,128)(2,1)} %rows_ref.1, s32[1,64]{1,0:T(1,128)} %bitcast.9, s32[1,128]{1,0:T(1,128)} %bitcast.10, s32[1,128]{1,0:T(1,128)} %bitcast.11, ...), custom_call_target="tpu_custom_call" | custom-call | tf_op jit(solution)/shard_map/pallas_call | solution.py:352
  120.6 0.0 copy-start
  120.6 10.1 %shard_map.78 = bf16[128,3,32,384]{3,2,1,0:T(8,128)(2,1)} custom-call(f32[3,128]{1,0:T(4,128)} %get-tuple-element.5.scale_ref, bf16[128,3,32,384]{3,2,1,0:T(8,128)(2,1)} %get-tuple-element.6.raw_ref), custom_call_target="tpu_custom_call" | custom-call | tf_op jit(solution)/shard_map/pallas_call | solution.py:419
  130.7 0.0 copy-done
  130.7 0.1 reshape.22
  130.8 0.7 copy.10
  (1 shorter events, 0.0 us)
Async XLA Ops:
  120.6 10.1 %copy-start = (f32[36,128]{1,0:T(8,128)S(1)}, f32[36,128]{1,0:T(8,128)}, u32[]{:S(2)}) copy-start(f32[36,128]{1,0:T(8,128)} %get-tuple-element.7) | copy-start | bytes 55300

commit v5 on v4

--- a/solution.py
+++ b/solution.py
@@ -18,7 +18,8 @@
 
 
 DAY_PARTS = 3
-AT_ONCE = 4
+PARTS = ((0, 0, 1), (1, 0, 1), (2, 0, 2), (2, 1, 2))
+AT_ONCE = 8
 
 
 def peer_at(me, step):
@@ -92,7 +93,7 @@
     me = lax.axis_index("key")
     other = {"feat": 1 - lax.axis_index("feat")}
     y, z, x = me // (NZ * NX), (me // NX) % NZ, me % NX
-    peers, feats, _ = landed.shape[1:]
+    peers, feats, _ = landed[0].shape
     keys = start_ref.shape[1]
     kinds = len(WINDOWS)
     load = pltpu.make_async_copy(rows_ref, held, load_sem)
@@ -125,20 +126,22 @@
     load.wait()
     pl.semaphore_wait(barrier, peers)
 
-    for part in range(DAY_PARTS):
-        days = slice(part * BLOCK, (part + 1) * BLOCK)
+    notes_at = len(PARTS)
+    for part, (day, piece, pieces) in enumerate(PARTS):
+        some = slice(piece * feats // pieces, (piece + 1) * feats // pieces)
+        days = slice(day * BLOCK, (day + 1) * BLOCK)
 
         def send(step, carry):
             peer = peer_at(me, step)
-            packed[part, step] = held[slot_ref[0, peer], :, days]
+            packed[part][step] = held[slot_ref[0, peer], some, days]
             where = {"key": peer}
-            send_to(packed.at[part, step], landed.at[part, me], send_sems.at[part], recv_sems.at[part], where)
+            send_to(packed[part].at[step], landed[part].at[me], send_sems.at[part], recv_sems.at[part], where)
             if part == 0:
-                send_to(note_ref.at[peer], note_landed.at[me], send_sems.at[DAY_PARTS], recv_sems.at[DAY_PARTS], where)
+                send_to(note_ref.at[peer], note_landed.at[me], send_sems.at[notes_at], recv_sems.at[notes_at], where)
             return carry
 
         lax.fori_loop(1, peers, send, 0)
-        landed[part, me] = held[slot_ref[0, me], :, days]
+        landed[part][me] = held[slot_ref[0, me], some, days]
     note_landed[me] = note_ref[me]
 
     shape = (2 * BLOCK, BLOCK)
@@ -169,7 +172,7 @@
             device_id_type=MESH,
         )
 
-    notes = whole(note_ref, note_landed, DAY_PARTS)
+    notes = whole(note_ref, note_landed, notes_at)
     notes.wait_recv()
     arrived = note_landed[:, 0, :BLOCK]
     receive = jnp.where(arrived == lane, 1.0, 0.0).T.astype(jnp.bfloat16)
@@ -201,47 +204,49 @@
         return copy
 
     writes = []
-    for part in range(DAY_PARTS):
-        arrival = whole(packed.at[part], landed.at[part], part)
+    for part, (day, piece, pieces) in enumerate(PARTS):
+        arrival = whole(packed[part], landed[part], part)
+        count_here = feats // pieces
+        first = piece * count_here
         arrival.wait_recv()
 
         def widen(some, carry):
-            spot = pl.ds(pl.multiple_of(some * 8 * feats, 8 * feats), 8 * feats)
-            piece = landed[part, pl.ds(some * 8, 8)].astype(jnp.float32)
-            wide[spot, :] = piece.reshape(8 * feats, BLOCK)
+            spot = pl.ds(pl.multiple_of(some * 8 * count_here, 8 * count_here), 8 * count_here)
+            piece = landed[part][pl.ds(some * 8, 8)].astype(jnp.float32)
+            wide[spot, :] = piece.reshape(8 * count_here, BLOCK)
             return carry
 
         lax.fori_loop(0, peers // 8, widen, 0)
-        live = lane + part * BLOCK >= start
+        live = lane + day * BLOCK >= start
 
         def features(group, carry):
             columns = []
             for local in range(AT_ONCE):
                 f = group * AT_ONCE + local
-                columns.append(wide[pl.ds(f, peers, stride=feats), :].astype(jnp.bfloat16))
+                columns.append(wide[pl.ds(f, peers, stride=count_here), :].astype(jnp.bfloat16))
             summed = jnp.dot(receive, jnp.concatenate(columns, axis=1), preferred_element_type=jnp.float32)
             results = []
             for local in range(AT_ONCE):
-                f = group * AT_ONCE + local
+                f = first + group * AT_ONCE + local
                 daily = summed[:, local * BLOCK : (local + 1) * BLOCK]
                 daily = jnp.where(live, daily, 0.0).astype(jnp.bfloat16)
-                if part == 0:
+                if day == 0:
                     result = jnp.dot(daily, bands[f, BLOCK:, :], preferred_element_type=jnp.float32)
                 else:
                     both = jnp.concatenate([before[f], daily], axis=1)
                     result = jnp.dot(both, bands[f], preferred_element_type=jnp.float32)
-                if part < DAY_PARTS - 1:
+                if day < DAY_PARTS - 1:
                     before[f] = daily
-                kept[f, part] = result.astype(jnp.bfloat16)
+                kept[f, day] = result.astype(jnp.bfloat16)
                 results.append(result)
             for w in range(kinds):
                 pieces = [result[:, w * BLOCK : (w + 1) * BLOCK] for result in results]
                 squares[w] += sum(piece * piece for piece in pieces)
             return carry
 
-        lax.fori_loop(0, feats // AT_ONCE, features, 0)
-        if part < DAY_PARTS - 1:
-            writes.append(pack(part))
+        lax.fori_loop(0, count_here // AT_ONCE, features, 0)
+        if day < DAY_PARTS - 1:
+            writes.append(pack(day))
 
     for w in range(kinds):
         share_out[w : w + 1, :] = jnp.sum(squares[w].T, axis=0, keepdims=True)
@@ -259,20 +264,6 @@
         low = (scaled - high.astype(jnp.float32)).astype(jnp.bfloat16)
         weights.append(jnp.concatenate([high, low], axis=0))
 
-    def add_cohorts(group, carry):
-        for local in range(AT_ONCE):
-            f = group * AT_ONCE + local
-            spot = pl.ds(pl.multiple_of(f * COHORTS, COHORTS), COHORTS)
-            for part in range(DAY_PARTS):
-                for w in range(kinds):
-                    lanes = slice(w * BLOCK, (w + 1) * BLOCK)
-                    result = jnp.dot(weights[w], kept[f, part, :, lanes], preferred_element_type=jnp.float32)
-                    both = result[:COHORTS] + result[COHORTS:]
-                    table[w, spot, part * BLOCK : (part + 1) * BLOCK] = both
-        return carry
-
-    lax.fori_loop(0, feats // AT_ONCE, add_cohorts, 0)
-
     def plane_peer(step):
         ty, tx = (y + step // NX) % NY, (x + step % NX) % NX
         return (ty * NZ + z) * NX + tx, ty * NX + tx
@@ -285,6 +276,19 @@
     each = order_ref.shape[0] // PLANE
     block_copies = []
     for w in range(kinds):
+        lanes = slice(w * BLOCK, (w + 1) * BLOCK)
+
+        def add_cohorts(group, carry):
+            for local in range(AT_ONCE):
+                f = group * AT_ONCE + local
+                spot = pl.ds(pl.multiple_of(f * COHORTS, COHORTS), COHORTS)
+                for day in range(DAY_PARTS):
+                    result = jnp.dot(weights[w], kept[f, day, :, lanes], preferred_element_type=jnp.float32)
+                    both = result[:COHORTS] + result[COHORTS:]
+                    table[w, spot, day * BLOCK : (day + 1) * BLOCK] = both
+            return carry
+
+        lax.fori_loop(0, feats // AT_ONCE, add_cohorts, 0)
         for g in range(rows // each):
             lines = table[w, g * BLOCK : (g + 1) * BLOCK, :].astype(jnp.bfloat16)
             by_day = lax.dot_general(
@@ -306,22 +310,24 @@
             block_copies[w * (PLANE - 1) + step - 1].wait_recv()
             total = total + block_in[w, step].astype(jnp.float32)
         sums[w * rows : (w + 1) * rows, :] = total
-    own_rows = mean_ref.shape[0]
+    own_rows, held_rows = mean_ref.shape[0], piece_out.shape[1]
+    filled = kinds * rows
+    sums[filled:, :] = jnp.zeros((held_rows * NZ - filled, BLOCK), jnp.float32)
     for tz in range(NZ):
-        piece_out[tz, :own_rows] = sums[pl.ds(tz, own_rows, stride=NZ), :]
+        piece_out[tz] = sums[pl.ds(tz, held_rows, stride=NZ), :].astype(jnp.bfloat16)
     piece_copies = []
     for step in range(1, NZ):
         peer, block = line_peer(step)
         sems = piece_sems.at[0, step], piece_sems.at[1, step]
         piece_copies.append(send_to(piece_out.at[block], piece_in.at[step], *sems, {"key": peer}))
-    total = piece_out[z, :own_rows]
+    total = piece_out[z].astype(jnp.float32)
     for step in range(1, NZ):
         piece_copies[step - 1].wait_recv()
-        total = total + piece_in[step, :own_rows]
-    mean_ref[...] = total / jnp.maximum(count, 1.0)
-
-    for part in range(DAY_PARTS):
-        whole(packed.at[part], landed.at[part], part).wait_send()
+        total = total + piece_in[step].astype(jnp.float32)
+    mean_ref[...] = total[:own_rows] / jnp.maximum(count, 1.0)
+
+    for part in range(len(PARTS)):
+        whole(packed[part], landed[part], part).wait_send()
     notes.wait_send()
     for copy in block_copies + piece_copies:
         copy.wait_send()
@@ -344,7 +350,7 @@
     lines = feats * COHORTS
     block_rows = lines // BLOCK * (days // PLANE)
     own_rows = kinds * block_rows // NZ
-    padded = -(-own_rows // 8) * 8
+    padded = -(-own_rows // 16) * 16
     vmem = pl.BlockSpec(memory_space=pltpu.VMEM)
     smem = pl.BlockSpec(memory_space=pltpu.SMEM)
     hbm = pl.BlockSpec(memory_space=pl.ANY)
@@ -363,8 +369,8 @@
             pltpu.VMEM((1, peers), jnp.int32),
             pltpu.SMEM((1, peers), jnp.int32),
             pltpu.VMEM((peers, 1, 2 * BLOCK), jnp.int32),
-            pltpu.VMEM((DAY_PARTS, peers, feats, BLOCK), half),
-            pltpu.VMEM((DAY_PARTS, peers, feats, BLOCK), half),
+            [pltpu.VMEM((peers, feats // n, BLOCK), half) for _, _, n in PARTS],
+            [pltpu.VMEM((peers, feats // n, BLOCK), half) for _, _, n in PARTS],
             pltpu.VMEM((peers, 1, 2 * BLOCK), jnp.int32),
             pltpu.VMEM((peers * feats, BLOCK), full),
             pltpu.VMEM((feats, 2 * BLOCK, kinds * BLOCK), half),
@@ -379,12 +385,12 @@
             pltpu.VMEM((PLANE, block_rows, BLOCK), full),
             pltpu.VMEM((kinds, PLANE, block_rows, BLOCK), half),
             pltpu.VMEM((kinds, PLANE, block_rows, BLOCK), half),
-            pltpu.VMEM((kinds * block_rows, BLOCK), full),
-            pltpu.VMEM((NZ, padded, BLOCK), full),
-            pltpu.VMEM((NZ, padded, BLOCK), full),
+            pltpu.VMEM((padded * NZ, BLOCK), full),
+            pltpu.VMEM((NZ, padded, BLOCK), half),
+            pltpu.VMEM((NZ, padded, BLOCK), half),
             pltpu.SemaphoreType.DMA,
-            pltpu.SemaphoreType.DMA((DAY_PARTS + 1,)),
-            pltpu.SemaphoreType.DMA((DAY_PARTS + 1,)),
+            pltpu.SemaphoreType.DMA((len(PARTS) + 1,)),
+            pltpu.SemaphoreType.DMA((len(PARTS) + 1,)),
             pltpu.SemaphoreType.DMA((2,)),
             pltpu.SemaphoreType.DMA((DAY_PARTS,)),
             pltpu.SemaphoreType.DMA((2, kinds, PLANE)),
@@ -403,25 +409,53 @@
     )
 
 
-def scale_kernel(scale_ref, raw_ref, out_ref):
-    block, kinds = raw_ref.shape[:2]
-    step = pl.program_id(0)
-    for local in range(block):
-        for w in range(kinds):
-            value = raw_ref[local, w].astype(jnp.float32) * scale_ref[w, step * block + local]
-            out_ref[local, w] = value.astype(jnp.bfloat16)
+def scale_kernel(scale_ref, raw_ref, out_ref, taken, given, in_sems, out_sems):
+    keys, kinds = taken.shape[:2]
+    parts = in_sems.shape[0]
+    block = keys // parts
+
+    def spot(part):
+        return pl.ds(part * block, block)
+
+    def read(part):
+        return pltpu.make_async_copy(raw_ref.at[spot(part)], taken.at[spot(part)], in_sems.at[part])
+
+    def write(part):
+        return pltpu.make_async_copy(given.at[spot(part)], out_ref.at[spot(part)], out_sems.at[part])
+
+    for part in range(parts):
+        read(part).start()
+    for part in range(parts):
+        read(part).wait()
+
+        def pair(index, carry):
+            for local in range(2):
+                key = part * block + index * 2 + local
+                for w in range(kinds):
+                    value = taken[key, w].astype(jnp.float32) * scale_ref[w, key]
+                    given[key, w] = value.astype(jnp.bfloat16)
+            return carry
+
+        lax.fori_loop(0, block // 2, pair, 0)
+        write(part).start()
+    for part in range(parts):
+        write(part).wait()
 
 
 def scale(raw, norm_scale):
-    keys, kinds, feats, days = raw.shape
-    block = 16
-    spec = pl.BlockSpec((block, kinds, feats, days), lambda i: (i, 0, 0, 0))
+    hbm = pl.BlockSpec(memory_space=pl.ANY)
+    parts = 8
     return pl.pallas_call(
         scale_kernel,
-        grid=(keys // block,),
         out_shape=jax.ShapeDtypeStruct(raw.shape, jnp.bfloat16),
-        in_specs=[pl.BlockSpec(memory_space=pltpu.SMEM), spec],
-        out_specs=spec,
+        in_specs=[pl.BlockSpec(memory_space=pltpu.SMEM), hbm],
+        out_specs=hbm,
+        scratch_shapes=[
+            pltpu.VMEM(raw.shape, jnp.bfloat16),
+            pltpu.VMEM(raw.shape, jnp.bfloat16),
+            pltpu.SemaphoreType.DMA((parts,)),
+            pltpu.SemaphoreType.DMA((parts,)),
+        ],
         compiler_params=pltpu.CompilerParams(vmem_limit_bytes=60 << 20),
     )(norm_scale, raw)
 

time: 133 us -> 126 us (0.947)
  Pallas kernels: 130 us -> 123 us
    pallas_call x1, Pallas kernels: 120 us -> 115 us  [main(): pl.pallas_call(main_kernel, out_shape=(jax.ShapeDtypeStruct((keys, kinds,...]
    pallas_call x1, Pallas kernels: 10.1 us -> 8.33 us  [scale(): pl.pallas_call(scale_kernel, out_shape=jax.ShapeDtypeStruct(raw.shape, jn...]
where the time goes in v5:
time: 126 us; the launch traced here: 125 us
  Pallas kernels  123 us (98%)
    pallas_call x1, Pallas kernels, main(): pl.pallas_call(main_kernel, out_shape=(jax.ShapeDtypeStruct((keys, kinds,...  115 us
    pallas_call x1, Pallas kernels, scale(): pl.pallas_call(scale_kernel, out_shape=jax.ShapeDtypeStruct(raw.shape, jn...  8.33 us

profile of v5, /device:TPU:2, one launch (start us, length us, event | category | flops | bytes accessed | tf_op | source)
XLA Modules:
  0.0 124.6 jit_solution(6009639584820369571)
XLA Ops:
  0.6 114.7 %shard_map.77 = (bf16[128,3,32,384]{3,2,1,0:T(8,128)(2,1)}, f32[3,128]{1,0:T(4,128)}, f32[36,128]{1,0:T(8,128)}) custom-call(f32[3,32]{1,0:T(4,128)} %rate_ref.1, bf16[64,32,384]{2,1,0:T(8,128)(2,1)} %rows_ref.1, s32[1,64]{1,0:T(1,128)} %bitcast.9, s32[1,128]{1,0:T(1,128)} %bitcast.10, s32[1,128]{1,0:T(1,128)} %bitcast.11, ...), custom_call_target="tpu_custom_call" | custom-call | tf_op jit(solution)/shard_map/pallas_call | solution.py:358
  115.4 0.0 copy-start
  115.4 8.3 %shard_map.78 = bf16[128,3,32,384]{3,2,1,0:T(8,128)(2,1)} custom-call(f32[3,128]{1,0:T(4,128)} %get-tuple-element.5.scale_ref, bf16[128,3,32,384]{3,2,1,0:T(8,128)(2,1)} %get-tuple-element.6.raw_ref), custom_call_target="tpu_custom_call" | custom-call | tf_op jit(solution)/shard_map/pallas_call | solution.py:448
  123.7 0.0 copy-done
  123.7 0.1 reshape.22
  123.8 0.7 copy.10
  (1 shorter events, 0.0 us)
Async XLA Ops:
  115.4 8.4 %copy-start = (f32[36,128]{1,0:T(8,128)S(1)}, f32[36,128]{1,0:T(8,128)}, u32[]{:S(2)}) copy-start(f32[36,128]{1,0:T(8,128)} %get-tuple-element.7) | copy-start | bytes 55300

commit v6 on v5

--- a/solution.py
+++ b/solution.py
@@ -78,7 +78,9 @@
     table,
     turned,
     block_out,
-    block_in,
+    first_in,
+    middle,
+    second_in,
     sums,
     piece_out,
     piece_in,
@@ -178,7 +180,7 @@
     receive = jnp.where(arrived == lane, 1.0, 0.0).T.astype(jnp.bfloat16)
     count = jnp.sum(note_landed[:, 0, BLOCK:], axis=0, keepdims=True).astype(jnp.float32)
 
-    def pack(part):
+    def interleave_day(part):
         def interleave(f, carry):
             for w in range(kinds):
                 piece = kept[f, part, :, w * BLOCK : (w + 1) * BLOCK].astype(jnp.float32)
@@ -187,6 +189,7 @@
 
         lax.fori_loop(0, feats, interleave, 0, unroll=2)
 
+    def pack(part):
         def some_keys(some, carry):
             for w in range(kinds):
                 spot = pl.ds(pl.multiple_of(some * 4 * feats, 4 * feats), 4 * feats)
@@ -246,6 +249,7 @@
 
         lax.fori_loop(0, count_here // AT_ONCE, features, 0)
         if day < DAY_PARTS - 1:
+            interleave_day(day)
             writes.append(pack(day))
 
     for w in range(kinds):
@@ -264,17 +268,23 @@
         low = (scaled - high.astype(jnp.float32)).astype(jnp.bfloat16)
         weights.append(jnp.concatenate([high, low], axis=0))
 
-    def plane_peer(step):
-        ty, tx = (y + step // NX) % NY, (x + step % NX) % NX
-        return (ty * NZ + z) * NX + tx, ty * NX + tx
+    def column_peer(step):
+        ty = (y + step) % NY
+        return (ty * NZ + z) * NX + x, ty
+
+    def row_peer(step):
+        tx = (x + step) % NX
+        return (y * NZ + z) * NX + tx, tx
 
     def line_peer(step):
         tz = (z + step) % NZ
         return (y * NZ + tz) * NX + x, tz
 
-    rows = block_out.shape[2]
+    rows = block_out.shape[3]
+    half = rows // 2
+    upper, lower = pl.ds(0, half), pl.ds(half, half)
     each = order_ref.shape[0] // PLANE
-    block_copies = []
+    first_copies, second_copies = [], []
     for w in range(kinds):
         lanes = slice(w * BLOCK, (w + 1) * BLOCK)
 
@@ -295,21 +305,45 @@
                 order_ref[...], lines, (((1,), (1,)), ((), ())), preferred_element_type=jnp.float32
             )
             turned[:, g * each : (g + 1) * each, :] = by_day.reshape(PLANE, each, BLOCK)
-        block_out[w] = turned[...].astype(jnp.bfloat16)
-        for step in range(1, PLANE):
-            peer, block = plane_peer(step)
-            sems = block_sems.at[0, w, step], block_sems.at[1, w, step]
-            block_copies.append(
-                send_to(block_out.at[w, block], block_in.at[w, step], *sems, {"key": peer})
-            )
+        block_out[w] = turned[...].astype(jnp.bfloat16).reshape(block_out.shape[1:])
+        for step in range(1, NX):
+            peer, place = row_peer(step)
+            sems = block_sems.at[0, w, 0, step], block_sems.at[1, w, 0, step]
+            source = block_out.at[w, :, place, upper]
+            first_copies.append(send_to(source, first_in.at[w, 0, step], *sems, {"key": peer}))
+            peer, place = column_peer(step)
+            sems = block_sems.at[0, w, 1, step], block_sems.at[1, w, 1, step]
+            source = block_out.at[w, place, :, lower]
+            first_copies.append(send_to(source, first_in.at[w, 1, step], *sems, {"key": peer}))
+    interleave_day(DAY_PARTS - 1)
+    for w in range(kinds):
+        for copy in first_copies[w * 2 * (NX - 1) : (w + 1) * 2 * (NX - 1)]:
+            copy.wait_recv()
+        for side in range(2):
+            own = block_out[w, :, x, :half] if side == 0 else block_out[w, y, :, half:]
+            total = own.astype(jnp.float32)
+            for step in range(1, NX):
+                total = total + first_in[w, side, step].astype(jnp.float32)
+            middle[w, side] = total.astype(jnp.bfloat16)
+        for step in range(1, NX):
+            peer, place = column_peer(step)
+            sems = block_sems.at[0, w, 2, step], block_sems.at[1, w, 2, step]
+            source = middle.at[w, 0, place]
+            second_copies.append(send_to(source, second_in.at[w, 0, step], *sems, {"key": peer}))
+            peer, place = row_peer(step)
+            sems = block_sems.at[0, w, 3, step], block_sems.at[1, w, 3, step]
+            source = middle.at[w, 1, place]
+            second_copies.append(send_to(source, second_in.at[w, 1, step], *sems, {"key": peer}))
     writes[0].wait()
     last_write = pack(DAY_PARTS - 1)
     for w in range(kinds):
-        total = block_out[w, y * NX + x].astype(jnp.float32)
-        for step in range(1, PLANE):
-            block_copies[w * (PLANE - 1) + step - 1].wait_recv()
-            total = total + block_in[w, step].astype(jnp.float32)
-        sums[w * rows : (w + 1) * rows, :] = total
+        for copy in second_copies[w * 2 * (NX - 1) : (w + 1) * 2 * (NX - 1)]:
+            copy.wait_recv()
+        for side, place in ((0, y), (1, x)):
+            total = middle[w, side, place].astype(jnp.float32)
+            for step in range(1, NX):
+                total = total + second_in[w, side, step].astype(jnp.float32)
+            sums[w * rows + side * half : w * rows + (side + 1) * half, :] = total
     own_rows, held_rows = mean_ref.shape[0], piece_out.shape[1]
     filled = kinds * rows
     sums[filled:, :] = jnp.zeros((held_rows * NZ - filled, BLOCK), jnp.float32)
@@ -329,7 +363,7 @@
     for part in range(len(PARTS)):
         whole(packed[part], landed[part], part).wait_send()
     notes.wait_send()
-    for copy in block_copies + piece_copies:
+    for copy in first_copies + second_copies + piece_copies:
         copy.wait_send()
     writes[1].wait()
     last_write.wait()
@@ -383,8 +417,10 @@
             pltpu.VMEM((kinds, keys), full),
             pltpu.VMEM((kinds, lines, days), full),
             pltpu.VMEM((PLANE, block_rows, BLOCK), full),
-            pltpu.VMEM((kinds, PLANE, block_rows, BLOCK), half),
-            pltpu.VMEM((kinds, PLANE, block_rows, BLOCK), half),
+            pltpu.VMEM((kinds, NY, NX, block_rows, BLOCK), half),
+            pltpu.VMEM((kinds, 2, NX, NY, block_rows // 2, BLOCK), half),
+            pltpu.VMEM((kinds, 2, NY, block_rows // 2, BLOCK), half),
+            pltpu.VMEM((kinds, 2, NX, block_rows // 2, BLOCK), half),
             pltpu.VMEM((padded * NZ, BLOCK), full),
             pltpu.VMEM((NZ, padded, BLOCK), half),
             pltpu.VMEM((NZ, padded, BLOCK), half),
@@ -393,7 +429,7 @@
             pltpu.SemaphoreType.DMA((len(PARTS) + 1,)),
             pltpu.SemaphoreType.DMA((2,)),
             pltpu.SemaphoreType.DMA((DAY_PARTS,)),
-            pltpu.SemaphoreType.DMA((2, kinds, PLANE)),
+            pltpu.SemaphoreType.DMA((2, kinds, 4, NX)),
             pltpu.SemaphoreType.DMA((2, NZ)),
         ],
         compiler_params=pltpu.CompilerParams(
@@ -429,14 +465,14 @@
         read(part).wait()
 
         def pair(index, carry):
-            for local in range(2):
-                key = part * block + index * 2 + local
+            for local in range(4):
+                key = part * block + index * 4 + local
                 for w in range(kinds):
                     value = taken[key, w].astype(jnp.float32) * scale_ref[w, key]
                     given[key, w] = value.astype(jnp.bfloat16)
             return carry
 
-        lax.fori_loop(0, block // 2, pair, 0)
+        lax.fori_loop(0, block // 4, pair, 0)
         write(part).start()
     for part in range(parts):
         write(part).wait()
@@ -444,7 +480,7 @@
 
 def scale(raw, norm_scale):
     hbm = pl.BlockSpec(memory_space=pl.ANY)
-    parts = 8
+    parts = 16
     return pl.pallas_call(
         scale_kernel,
         out_shape=jax.ShapeDtypeStruct(raw.shape, jnp.bfloat16),

time: 126 us -> 124 us (0.984)
    pallas_call x1, Pallas kernels: 115 us -> 113 us  [main(): pl.pallas_call(main_kernel, out_shape=(jax.ShapeDtypeStruct((keys, kinds,...]
where the time goes in v6:
time: 124 us; the launch traced here: 123 us
  Pallas kernels  122 us (98%)
    pallas_call x1, Pallas kernels, main(): pl.pallas_call(main_kernel, out_shape=(jax.ShapeDtypeStruct((keys, kinds,...  113 us
    pallas_call x1, Pallas kernels, scale(): pl.pallas_call(scale_kernel, out_shape=jax.ShapeDtypeStruct(raw.shape, jn...  8.08 us

profile of v6, /device:TPU:2, one launch (start us, length us, event | category | flops | bytes accessed | tf_op | source)
XLA Modules:
  0.0 123.0 jit_solution(15077705408151792570)
XLA Ops:
  0.6 113.4 %shard_map.77 = (bf16[128,3,32,384]{3,2,1,0:T(8,128)(2,1)}, f32[3,128]{1,0:T(4,128)}, f32[36,128]{1,0:T(8,128)}) custom-call(f32[3,32]{1,0:T(4,128)} %rate_ref.1, bf16[64,32,384]{2,1,0:T(8,128)(2,1)} %rows_ref.1, s32[1,64]{1,0:T(1,128)} %bitcast.9, s32[1,128]{1,0:T(1,128)} %bitcast.10, s32[1,128]{1,0:T(1,128)} %bitcast.11, ...), custom_call_target="tpu_custom_call" | custom-call | tf_op jit(solution)/shard_map/pallas_call | solution.py:392
  114.1 0.0 copy-start
  114.1 8.1 %shard_map.78 = bf16[128,3,32,384]{3,2,1,0:T(8,128)(2,1)} custom-call(f32[3,128]{1,0:T(4,128)} %get-tuple-element.5.scale_ref, bf16[128,3,32,384]{3,2,1,0:T(8,128)(2,1)} %get-tuple-element.6.raw_ref), custom_call_target="tpu_custom_call" | custom-call | tf_op jit(solution)/shard_map/pallas_call | solution.py:484
  122.2 0.0 copy-done
  122.2 0.1 reshape.22
  122.3 0.7 copy.10
  (1 shorter events, 0.0 us)
Async XLA Ops:
  114.1 8.1 %copy-start = (f32[36,128]{1,0:T(8,128)S(1)}, f32[36,128]{1,0:T(8,128)}, u32[]{:S(2)}) copy-start(f32[36,128]{1,0:T(8,128)} %get-tuple-element.7) | copy-start | bytes 55300
